TPU v7x, 256 devices: a whole 4x4x8 slice. The times are simulated.
256 devices in a mesh: gx: 4 (over y), gy: 8 (over z_lo, x), gz: 8 (over z_hi, core).
Axes of the slice: x: 4, y: 4, z: 8 (z_hi: 4, z_lo: 2; z = z_hi * 2 + z_lo), core: 2. Of those that a mesh axis runs over, the one named last changes fastest.
Arguments:
- unary_q: int32 [32, 64, 64, 128], P('gx', 'gy', 'gz'), may hold values from -127 to 127
- potential_q: int32 [128, 128], replicated, may hold values from -127 to 127
- belief_grad: bfloat16 [32, 64, 64, 128], P('gx', 'gy', 'gz'), may hold values from -6 to 6
Outputs:
- unary_grad: float32 [32, 64, 64, 128], P('gx', 'gy', 'gz')
- potential_grad: float32 [128, 128], replicated
All inputs are finite; a program needn't handle non-finite values.
Results may differ from a plain program's by a relative error of at most 0.008.
Values may be sent and summed in bfloat16 or wider, within the bound.
A program may use at most 64 MiB of HBM per device.

v0:
```python
import math

import jax
import jax.numpy as jnp
from jax import lax
from jax.sharding import PartitionSpec as P

ITERS = 3


OPPOSITE = (1, 0, 3, 2, 5, 4)


def from_behind(value, axis, steps):
    count = lax.axis_size(axis)
    first, last = (max(0, -steps), min(count, count - steps))
    return lax.ppermute(value, axis, [(source, source + steps) for source in range(first, last)])


def with_halo(block, sides, width):
    for axis, dim in sides:
        count = lax.axis_size(axis)
        forward = [(i, i + 1) for i in range(count - 1)]
        backward = [(target, source) for source, target in forward]
        low = lax.ppermute(
            lax.slice_in_dim(block, block.shape[dim] - width, None, axis=dim), axis, forward
        )
        high = lax.ppermute(lax.slice_in_dim(block, 0, width, axis=dim), axis, backward)
        block = jnp.concatenate([low, block, high], axis=dim)
    return block


def layers(values, spatial, begin_at, end_at):
    return lax.slice_in_dim(values, begin_at, end_at, axis=spatial)


def project(operand, table):
    out_shape = operand.shape[:-1] + (table.shape[1],)
    result = jnp.dot(
        operand.reshape(-1, operand.shape[-1]), table, preferred_element_type=jnp.float32
    )
    return result.reshape(out_shape)


def normalized(cavity, pair_table):
    scores = project(cavity, pair_table)
    totals = jnp.sum(scores, axis=-1, keepdims=True)
    return (scores, totals)


def cell_product(unary_factor, incoming):
    product = unary_factor
    for direction in range(6):
        product = product * incoming[direction].astype(jnp.float32)
    return product


def move_face(layer_slab, spatial, offset):
    if spatial == 0:
        return from_behind(layer_slab, "gx", offset)
    if spatial == 1:
        return from_behind(layer_slab, "gy", offset)
    return from_behind(layer_slab, "gz", offset)


def with_fill(arrived, at_edge):
    return jnp.where(at_edge, jnp.ones_like(arrived), arrived)


def rim_of(padded, spatial, upper_side):
    slicers = []
    for axis_pos in range(3):
        if axis_pos == spatial:
            position = padded.shape[axis_pos] - 1 if upper_side else 0
            slicers.append(slice(position, position + 1))
        else:
            slicers.append(slice(1, padded.shape[axis_pos] - 1))
    slicers.append(slice(0, padded.shape[3]))
    return padded[tuple(slicers)]


def pass_products(outgoing, previous, product, pair_table, lower_edge, upper_edge):
    padded = with_halo(product.astype(jnp.bfloat16), (("gx", 0), ("gy", 1), ("gz", 2)), 1).astype(
        product.dtype
    )
    labels = product.shape[-1]
    result = []
    for direction in range(6):
        spatial = direction // 2
        source = outgoing[direction]
        extent = source.shape[spatial]
        upper_side = direction % 2 == 1
        at_edge = upper_edge[spatial] if upper_side else lower_edge[spatial]
        remote = rim_of(padded, spatial, upper_side)
        remote = jnp.where(at_edge, jnp.ones_like(remote), remote)
        if previous is None:
            cavity = remote.astype(jnp.bfloat16)
        else:
            own_out = previous[OPPOSITE[direction]]
            if upper_side:
                nearest = layers(own_out, spatial, extent - 1, extent)
            else:
                nearest = layers(own_out, spatial, 0, 1)
            cavity = (remote / nearest.astype(jnp.float32)).astype(jnp.bfloat16)
        scores, totals = normalized(cavity, pair_table)
        arrived = with_fill((labels * scores / totals).astype(jnp.bfloat16), at_edge)
        if upper_side:
            result.append(
                jnp.concatenate([layers(source, spatial, 1, extent), arrived], axis=spatial)
            )
        else:
            result.append(
                jnp.concatenate([arrived, layers(source, spatial, 0, extent - 1)], axis=spatial)
            )
    return result


def return_gradients(gradients):
    result = []
    for direction in range(6):
        spatial = direction // 2
        source = gradients[direction]
        extent = source.shape[spatial]
        if direction % 2 == 0:
            arrived = move_face(layers(source, spatial, 0, 1), spatial, -1)
            result.append(
                jnp.concatenate([layers(source, spatial, 1, extent), arrived], axis=spatial)
            )
        else:
            arrived = move_face(layers(source, spatial, extent - 1, extent), spatial, 1)
            result.append(
                jnp.concatenate([arrived, layers(source, spatial, 0, extent - 1)], axis=spatial)
            )
    return result


def cavities(product, incoming):
    if incoming is None:
        return (product.astype(jnp.bfloat16)[None], None)
    opposite = jnp.stack([incoming[OPPOSITE[direction]] for direction in range(6)]).astype(
        jnp.float32
    )
    return ((product[None] / opposite).astype(jnp.bfloat16), opposite)


def on_device(unary_q, potential_q, belief_grad):
    unary_factor = jnp.exp(unary_q.astype(jnp.float32) / 32.0)
    pair_factor = jnp.exp(potential_q.astype(jnp.float32) / 64.0)
    pair_table = pair_factor.astype(jnp.bfloat16)
    labels = unary_factor.shape[-1]
    lower_edge = (lax.axis_index("gx") == 0, lax.axis_index("gy") == 0, lax.axis_index("gz") == 0)
    upper_edge = (
        lax.axis_index("gx") == lax.axis_size("gx") - 1,
        lax.axis_index("gy") == lax.axis_size("gy") - 1,
        lax.axis_index("gz") == lax.axis_size("gz") - 1,
    )
    history = [None]
    incoming = None
    previous = None
    for iteration in range(ITERS):
        if incoming is None:
            product = unary_factor
        else:
            product = cell_product(unary_factor, incoming)
        cavity, opposite = cavities(product, incoming)
        scores, totals = normalized(cavity, pair_table)
        messages = (labels * scores / totals).astype(jnp.bfloat16)
        outgoing = [messages[direction if messages.shape[0] > 1 else 0] for direction in range(6)]
        incoming = pass_products(outgoing, previous, product, pair_table, lower_edge, upper_edge)
        previous = outgoing
        history.append(incoming)
    product = cell_product(unary_factor, incoming)
    belief = product / jnp.sum(product, axis=-1, keepdims=True)
    target = belief_grad.astype(jnp.float32)
    unary_grad = target - belief * jnp.sum(target, axis=-1, keepdims=True)
    gradients = [
        (unary_grad / incoming[direction].astype(jnp.float32)).astype(jnp.bfloat16)
        for direction in range(6)
    ]
    combined = jnp.zeros((labels, labels), jnp.float32)
    for iteration in range(ITERS, 0, -1):
        returned = return_gradients(gradients)
        before = history[iteration - 1]
        if before is None:
            product = unary_factor
        else:
            product = cell_product(unary_factor, before)
        cavity, opposite = cavities(product, before)
        scores, totals = normalized(cavity, pair_table)
        back_grad = jnp.stack(returned).astype(jnp.float32)
        weight = jnp.sum(back_grad * scores, axis=-1, keepdims=True) / totals
        score_grad = (labels / totals * (back_grad - weight)).astype(jnp.bfloat16)
        cavity_grad = project(score_grad, pair_table.T)
        spread = jnp.broadcast_to(cavity, score_grad.shape).reshape(-1, labels)
        pair_term = lax.dot_general(
            spread,
            score_grad.reshape(-1, labels),
            (((0,), (0,)), ((), ())),
            preferred_element_type=jnp.float32,
        )
        if before is None:
            product_grad = jnp.sum(cavity_grad, axis=0)
        else:
            product_grad = jnp.sum(cavity_grad / opposite, axis=0)
        unary_grad = unary_grad + product_grad * product
        if before is not None:
            gradients = [
                (
                    product
                    / before[direction].astype(jnp.float32)
                    * (
                        product_grad
                        - cavity_grad[OPPOSITE[direction]] / before[direction].astype(jnp.float32)
                    )
                ).astype(jnp.bfloat16)
                for direction in range(6)
            ]
        combined = combined + pair_term
    combined = lax.psum(combined, ("gx", "gy", "gz"))
    cell_count = (
        unary_q.shape[0]
        * unary_q.shape[1]
        * unary_q.shape[2]
        * lax.axis_size("gx")
        * lax.axis_size("gy")
        * lax.axis_size("gz")
    )
    potential_grad = pair_factor * combined * (labels / math.sqrt(cell_count))
    return (unary_grad, potential_grad)


def solution(mesh):
    return jax.shard_map(
        on_device,
        mesh=mesh,
        in_specs=(P("gx", "gy", "gz", None), P(), P("gx", "gy", "gz", None)),
        out_specs=(P("gx", "gy", "gz", None), P()),
        check_vma=False,
    )
```

profile of v0, /device:TPU:1, one launch (start us, length us, event | category | flops | bytes accessed | tf_op | source)
XLA Modules:
  0.0 479.8 jit_solution(9949245999855717641)
XLA Ops:
  8.3 4.0 collective-permute-start
  16.8 3.1 collective-permute-start.2
  21.3 3.2 collective-permute-done.3
  24.6 8.3 %collective-permute-start.4 = (bf16[10,10,1,128]{3,2,1,0:T(2,128)(2,1)S(1)}, bf16[10,10,1,128]{3,2,1,0:T(2,128)(2,1)S(1)}, u32[]{:S(2)}, u32[]{:S(2)}) collective-permute-start(bf16[10,10,1,128]{3,2,1,0:T(2,128)(2,1)S(1)} %get-tuple-element.58), channel_id=1, source_target_pairs={{0,1},{1,2},{2,3},{3,4},{4,5},{5,6},{6,7},{8,9},{9,10},{10,11},{11... | collective-permute-start | bytes 76808 | tf_op jit(solution)/shard_map/ppermute | solution.py:25
  34.9 4.3 collective-permute-done.5
  42.7 3.2 collective-permute-start.6
  50.4 3.1 collective-permute-start.8
  54.9 3.1 collective-permute-done.9
  58.1 5.7 %collective-permute-start.10 = (bf16[10,10,1,128]{3,2,1,0:T(2,128)(2,1)S(1)}, bf16[10,10,1,128]{3,2,1,0:T(2,128)(2,1)S(1)}, u32[]{:S(2)}, u32[]{:S(2)}) collective-permute-start(bf16[10,10,1,128]{3,2,1,0:T(2,128)(2,1)S(1)} %get-tuple-element.56), channel_id=1, source_target_pairs={{0,1},{1,2},{2,3},{3,4},{4,5},{5,6},{6,7},{8,9},{9,10},{10,11},{11... | collective-permute-start | bytes 76808 | tf_op jit(solution)/shard_map/ppermute | solution.py:25
  65.9 4.2 collective-permute-done.11
  73.5 2.9 collective-permute-start.12
  80.9 3.9 collective-permute-start.14
  86.8 2.8 collective-permute-done.15
  89.7 5.7 %collective-permute-start.16 = (bf16[10,10,1,128]{3,2,1,0:T(2,128)(2,1)S(1)}, bf16[10,10,1,128]{3,2,1,0:T(2,128)(2,1)S(1)}, u32[]{:S(2)}, u32[]{:S(2)}) collective-permute-start(bf16[10,10,1,128]{3,2,1,0:T(2,128)(2,1)S(1)} %get-tuple-element.54), channel_id=1, source_target_pairs={{0,1},{1,2},{2,3},{3,4},{4,5},{5,6},{6,7},{8,9},{9,10},{10,11},{11... | collective-permute-start | bytes 76808 | tf_op jit(solution)/shard_map/ppermute | solution.py:25
  104.0 2.1 fusion.262
  106.1 2.1 fusion.261
  108.2 2.1 fusion.259
  117.3 2.2 fusion.244
  120.8 2.2 fusion.245
  129.5 10.5 %fusion.33 = (bf16[8,8,8,128]{3,2,1,0:T(8,128)(2,1)S(1)}, bf16[8,8,8,128]{3,2,1,0:T(8,128)(2,1)S(1)}, bf16[8,8,8,128]{3,2,1,0:T(8,128)(2,1)S(1)}, bf16[8,8,8,128...) fusion(bf16[8,8,1,128]{3,2,1,0:T(2,128)(2,1)S(1)} %broadcast_se, ...), kind=kOutput, calls=%fused_computation.101 | output fusion | flops 4719231 | bytes 2490368 | tf_op jit(solution)/shard_map/div | solution.py:173
  142.1 4.0 collective-permute-start.19
  147.4 4.4 collective-permute-start.21
  153.8 4.7 collective-permute-start.23
  160.6 2.7 fusion.10
  167.4 4.0 collective-permute-start.25
  172.7 4.3 collective-permute-start.27
  178.9 6.1 %collective-permute-start.29 = (bf16[8,8,1,128]{3,2,1,0:T(2,128)(2,1)S(1)}, bf16[8,8,1,128]{3,2,1,0:T(2,128)(2,1)S(1)}, u32[]{:S(2)}, u32[]{:S(2)}) collective-permute-start(bf16[8,8,1,128]{3,2,1,0:T(2,128)(2,1)S(1)} %slice.628), channel_id=1, source_target_pairs={{0,1},{1,2},{2,3},{3,4},{4,5},{5,6},{6,7},{8,9},{9,10},{10,11},{11... | collective-permute-start | bytes 49160 | tf_op jit(solution)/shard_map/ppermute | solution.py:17
  186.8 2.4 convolution_bitcast_fusion.1
  195.1 4.0 collective-permute-start.31
  200.4 4.4 collective-permute-start.33
  206.7 6.2 %collective-permute-start.35 = (bf16[8,8,1,128]{3,2,1,0:T(2,128)(2,1)S(1)}, bf16[8,8,1,128]{3,2,1,0:T(2,128)(2,1)S(1)}, u32[]{:S(2)}, u32[]{:S(2)}) collective-permute-start(bf16[8,8,1,128]{3,2,1,0:T(2,128)(2,1)S(1)} %slice.646), channel_id=1, source_target_pairs={{0,1},{1,2},{2,3},{3,4},{4,5},{5,6},{6,7},{8,9},{9,10},{10,11},{11... | collective-permute-start | bytes 49160 | tf_op jit(solution)/shard_map/ppermute | solution.py:17
  219.6 251.9 %all-reduce.2.cloned.1.call-done = f32[128,128]{1,0:T(8,128)} async-done(((f32[128,128]{1,0:T(8,128)}), f32[128,128]{1,0:T(8,128)}) %all-reduce.2.cloned.1.call-update) | async-done | bytes 65552 | tf_op jit(solution)/shard_map/psum | solution.py:219
  (384 shorter events, 85.6 us)
Async XLA Ops:
  7.2 464.3 %all-reduce.2.cloned.1.call-start = ((), (), s32[]{:S(2)}) async-start(), calls=%async_computation | async-start | bytes 131072 | tf_op jit(solution)/shard_map/psum | solution.py:219
  8.3 7.9 %collective-permute-start = (bf16[1,8,8,128]{3,2,1,0:T(8,128)(2,1)S(1)}, bf16[1,8,8,128]{3,2,1,0:T(8,128)(2,1)S(1)}, u32[]{:S(2)}, u32[]{:S(2)}) collective-permute-start(bf16[1,8,8,128]{3,2,1,0:T(8,128)(2,1)S(1)} %get-tuple-element.80), channel_id=1, source_target_pairs={{0,64},{64,128},{128,192},{1,65},{65,129},{129,193},{2,66},{66,130... | collective-permute-start | bytes 49160 | tf_op jit(solution)/shard_map/ppermute | solution.py:25
  19.9 4.5 collective-permute-start.3
  24.6 10.4 %collective-permute-start.4 = (bf16[10,10,1,128]{3,2,1,0:T(2,128)(2,1)S(1)}, bf16[10,10,1,128]{3,2,1,0:T(2,128)(2,1)S(1)}, u32[]{:S(2)}, u32[]{:S(2)}) collective-permute-start(bf16[10,10,1,128]{3,2,1,0:T(2,128)(2,1)S(1)} %get-tuple-element.58), channel_id=1, source_target_pairs={{0,1},{1,2},{2,3},{3,4},{4,5},{5,6},{6,7},{8,9},{9,10},{10,11},{11... | collective-permute-start | bytes 76808 | tf_op jit(solution)/shard_map/ppermute | solution.py:25
  32.9 6.3 %collective-permute-start.5 = (bf16[10,10,1,128]{3,2,1,0:T(2,128)(2,1)S(1)}, bf16[10,10,1,128]{3,2,1,0:T(2,128)(2,1)S(1)}, u32[]{:S(2)}, u32[]{:S(2)}) collective-permute-start(bf16[10,10,1,128]{3,2,1,0:T(2,128)(2,1)S(1)} %get-tuple-element.59), channel_id=1, source_target_pairs={{1,0},{2,1},{3,2},{4,3},{5,4},{6,5},{7,6},{9,8},{10,9},{11,10},{12... | collective-permute-start | bytes 76808 | tf_op jit(solution)/shard_map/ppermute | solution.py:28
  42.7 5.7 %collective-permute-start.6 = (bf16[1,8,8,128]{3,2,1,0:T(8,128)(2,1)S(1)}, bf16[1,8,8,128]{3,2,1,0:T(8,128)(2,1)S(1)}, u32[]{:S(2)}, u32[]{:S(2)}) collective-permute-start(bf16[1,8,8,128]{3,2,1,0:T(8,128)(2,1)S(1)} %get-tuple-element.72), channel_id=1, source_target_pairs={{0,64},{64,128},{128,192},{1,65},{65,129},{129,193},{2,66},{66,130... | collective-permute-start | bytes 49160 | tf_op jit(solution)/shard_map/ppermute | solution.py:25
  53.5 4.5 collective-permute-start.9
  58.1 7.8 %collective-permute-start.10 = (bf16[10,10,1,128]{3,2,1,0:T(2,128)(2,1)S(1)}, bf16[10,10,1,128]{3,2,1,0:T(2,128)(2,1)S(1)}, u32[]{:S(2)}, u32[]{:S(2)}) collective-permute-start(bf16[10,10,1,128]{3,2,1,0:T(2,128)(2,1)S(1)} %get-tuple-element.56), channel_id=1, source_target_pairs={{0,1},{1,2},{2,3},{3,4},{4,5},{5,6},{6,7},{8,9},{9,10},{10,11},{11... | collective-permute-start | bytes 76808 | tf_op jit(solution)/shard_map/ppermute | solution.py:25
  63.8 6.3 %collective-permute-start.11 = (bf16[10,10,1,128]{3,2,1,0:T(2,128)(2,1)S(1)}, bf16[10,10,1,128]{3,2,1,0:T(2,128)(2,1)S(1)}, u32[]{:S(2)}, u32[]{:S(2)}) collective-permute-start(bf16[10,10,1,128]{3,2,1,0:T(2,128)(2,1)S(1)} %get-tuple-element.57), channel_id=1, source_target_pairs={{1,0},{2,1},{3,2},{4,3},{5,4},{6,5},{7,6},{9,8},{10,9},{11,10},{12... | collective-permute-start | bytes 76808 | tf_op jit(solution)/shard_map/ppermute | solution.py:28
  73.5 6.0 %collective-permute-start.12 = (bf16[1,8,8,128]{3,2,1,0:T(8,128)(2,1)S(1)}, bf16[1,8,8,128]{3,2,1,0:T(8,128)(2,1)S(1)}, u32[]{:S(2)}, u32[]{:S(2)}) collective-permute-start(bf16[1,8,8,128]{3,2,1,0:T(8,128)(2,1)S(1)} %get-tuple-element.70), channel_id=1, source_target_pairs={{0,64},{64,128},{128,192},{1,65},{65,129},{129,193},{2,66},{66,130... | collective-permute-start | bytes 49160 | tf_op jit(solution)/shard_map/ppermute | solution.py:25
  80.9 5.8 %collective-permute-start.14 = (bf16[10,1,8,128]{3,2,1,0:T(8,128)(2,1)S(1)}, bf16[10,1,8,128]{3,2,1,0:T(8,128)(2,1)S(1)}, u32[]{:S(2)}, u32[]{:S(2)}) collective-permute-start(bf16[10,1,8,128]{3,2,1,0:T(8,128)(2,1)S(1)} %get-tuple-element.64), channel_id=1, source_target_pairs={{0,8},{8,16},{16,24},{24,32},{32,40},{40,48},{48,56},{1,9},{9,17},... | collective-permute-start | bytes 61448 | tf_op jit(solution)/shard_map/ppermute | solution.py:25
  84.8 4.8 %collective-permute-start.15 = (bf16[10,1,8,128]{3,2,1,0:T(8,128)(2,1)S(1)}, bf16[10,1,8,128]{3,2,1,0:T(8,128)(2,1)S(1)}, u32[]{:S(2)}, u32[]{:S(2)}) collective-permute-start(bf16[10,1,8,128]{3,2,1,0:T(8,128)(2,1)S(1)} %get-tuple-element.65), channel_id=1, source_target_pairs={{8,0},{16,8},{24,16},{32,24},{40,32},{48,40},{56,48},{9,1},{17,9},... | collective-permute-start | bytes 61448 | tf_op jit(solution)/shard_map/ppermute | solution.py:28
  89.7 10.3 %collective-permute-start.16 = (bf16[10,10,1,128]{3,2,1,0:T(2,128)(2,1)S(1)}, bf16[10,10,1,128]{3,2,1,0:T(2,128)(2,1)S(1)}, u32[]{:S(2)}, u32[]{:S(2)}) collective-permute-start(bf16[10,10,1,128]{3,2,1,0:T(2,128)(2,1)S(1)} %get-tuple-element.54), channel_id=1, source_target_pairs={{0,1},{1,2},{2,3},{3,4},{4,5},{5,6},{6,7},{8,9},{9,10},{10,11},{11... | collective-permute-start | bytes 76808 | tf_op jit(solution)/shard_map/ppermute | solution.py:25
  95.4 6.3 %collective-permute-start.17 = (bf16[10,10,1,128]{3,2,1,0:T(2,128)(2,1)S(1)}, bf16[10,10,1,128]{3,2,1,0:T(2,128)(2,1)S(1)}, u32[]{:S(2)}, u32[]{:S(2)}) collective-permute-start(bf16[10,10,1,128]{3,2,1,0:T(2,128)(2,1)S(1)} %get-tuple-element.55), channel_id=1, source_target_pairs={{1,0},{2,1},{3,2},{4,3},{5,4},{6,5},{7,6},{9,8},{10,9},{11,10},{12... | collective-permute-start | bytes 76808 | tf_op jit(solution)/shard_map/ppermute | solution.py:28
  140.0 13.8 %collective-permute-start.18 = (bf16[1,8,8,128]{3,2,1,0:T(8,128)(2,1)S(1)}, bf16[1,8,8,128]{3,2,1,0:T(8,128)(2,1)S(1)}, u32[]{:S(2)}, u32[]{:S(2)}) collective-permute-start(bf16[1,8,8,128]{3,2,1,0:T(8,128)(2,1)S(1)} %slice.601), channel_id=1, source_target_pairs={{64,0},{128,64},{192,128},{65,1},{129,65},{193,129},{66,2},{130,66... | collective-permute-start | bytes 49160 | tf_op jit(solution)/shard_map/ppermute | solution.py:17
  142.1 16.4 %collective-permute-start.19 = (bf16[1,8,8,128]{3,2,1,0:T(8,128)(2,1)S(1)}, bf16[1,8,8,128]{3,2,1,0:T(8,128)(2,1)S(1)}, u32[]{:S(2)}, u32[]{:S(2)}) collective-permute-start(bf16[1,8,8,128]{3,2,1,0:T(8,128)(2,1)S(1)} %slice.602), channel_id=1, source_target_pairs={{0,64},{64,128},{128,192},{1,65},{65,129},{129,193},{2,66},{66,130... | collective-permute-start | bytes 49160 | tf_op jit(solution)/shard_map/ppermute | solution.py:17
  146.1 12.5 %collective-permute-start.20 = (bf16[8,1,8,128]{3,2,1,0:T(8,128)(2,1)S(1)}, bf16[8,1,8,128]{3,2,1,0:T(8,128)(2,1)S(1)}, u32[]{:S(2)}, u32[]{:S(2)}) collective-permute-start(bf16[8,1,8,128]{3,2,1,0:T(8,128)(2,1)S(1)} %slice.605), channel_id=1, source_target_pairs={{8,0},{16,8},{24,16},{32,24},{40,32},{48,40},{56,48},{9,1},{17,9},... | collective-permute-start | bytes 49160 | tf_op jit(solution)/shard_map/ppermute | solution.py:17
  147.4 11.2 %collective-permute-start.21 = (bf16[8,1,8,128]{3,2,1,0:T(8,128)(2,1)S(1)}, bf16[8,1,8,128]{3,2,1,0:T(8,128)(2,1)S(1)}, u32[]{:S(2)}, u32[]{:S(2)}) collective-permute-start(bf16[8,1,8,128]{3,2,1,0:T(8,128)(2,1)S(1)} %slice.606), channel_id=1, source_target_pairs={{0,8},{8,16},{16,24},{24,32},{32,40},{40,48},{48,56},{1,9},{9,17},... | collective-permute-start | bytes 49160 | tf_op jit(solution)/shard_map/ppermute | solution.py:17
  151.8 6.9 %collective-permute-start.22 = (bf16[8,8,1,128]{3,2,1,0:T(2,128)(2,1)S(1)}, bf16[8,8,1,128]{3,2,1,0:T(2,128)(2,1)S(1)}, u32[]{:S(2)}, u32[]{:S(2)}) collective-permute-start(bf16[8,8,1,128]{3,2,1,0:T(2,128)(2,1)S(1)} %slice.609), channel_id=1, source_target_pairs={{1,0},{2,1},{3,2},{4,3},{5,4},{6,5},{7,6},{9,8},{10,9},{11,10},{12... | collective-permute-start | bytes 49160 | tf_op jit(solution)/shard_map/ppermute | solution.py:17
  153.8 5.6 %collective-permute-start.23 = (bf16[8,8,1,128]{3,2,1,0:T(2,128)(2,1)S(1)}, bf16[8,8,1,128]{3,2,1,0:T(2,128)(2,1)S(1)}, u32[]{:S(2)}, u32[]{:S(2)}) collective-permute-start(bf16[8,8,1,128]{3,2,1,0:T(2,128)(2,1)S(1)} %slice.610), channel_id=1, source_target_pairs={{0,1},{1,2},{2,3},{3,4},{4,5},{5,6},{6,7},{8,9},{9,10},{10,11},{11... | collective-permute-start | bytes 49160 | tf_op jit(solution)/shard_map/ppermute | solution.py:17
  165.3 13.6 %collective-permute-start.24 = (bf16[1,8,8,128]{3,2,1,0:T(8,128)(2,1)S(1)}, bf16[1,8,8,128]{3,2,1,0:T(8,128)(2,1)S(1)}, u32[]{:S(2)}, u32[]{:S(2)}) collective-permute-start(bf16[1,8,8,128]{3,2,1,0:T(8,128)(2,1)S(1)} %slice.614), channel_id=1, source_target_pairs={{64,0},{128,64},{192,128},{65,1},{129,65},{193,129},{66,2},{130,66... | collective-permute-start | bytes 49160 | tf_op jit(solution)/shard_map/ppermute | solution.py:17
  167.4 17.6 %collective-permute-start.25 = (bf16[1,8,8,128]{3,2,1,0:T(8,128)(2,1)S(1)}, bf16[1,8,8,128]{3,2,1,0:T(8,128)(2,1)S(1)}, u32[]{:S(2)}, u32[]{:S(2)}) collective-permute-start(bf16[1,8,8,128]{3,2,1,0:T(8,128)(2,1)S(1)} %slice.616), channel_id=1, source_target_pairs={{0,64},{64,128},{128,192},{1,65},{65,129},{129,193},{2,66},{66,130... | collective-permute-start | bytes 49160 | tf_op jit(solution)/shard_map/ppermute | solution.py:17
  171.4 13.7 %collective-permute-start.26 = (bf16[8,1,8,128]{3,2,1,0:T(8,128)(2,1)S(1)}, bf16[8,1,8,128]{3,2,1,0:T(8,128)(2,1)S(1)}, u32[]{:S(2)}, u32[]{:S(2)}) collective-permute-start(bf16[8,1,8,128]{3,2,1,0:T(8,128)(2,1)S(1)} %slice.620), channel_id=1, source_target_pairs={{8,0},{16,8},{24,16},{32,24},{40,32},{48,40},{56,48},{9,1},{17,9},... | collective-permute-start | bytes 49160 | tf_op jit(solution)/shard_map/ppermute | solution.py:17
  172.7 12.4 %collective-permute-start.27 = (bf16[8,1,8,128]{3,2,1,0:T(8,128)(2,1)S(1)}, bf16[8,1,8,128]{3,2,1,0:T(8,128)(2,1)S(1)}, u32[]{:S(2)}, u32[]{:S(2)}) collective-permute-start(bf16[8,1,8,128]{3,2,1,0:T(8,128)(2,1)S(1)} %slice.622), channel_id=1, source_target_pairs={{0,8},{8,16},{16,24},{24,32},{32,40},{40,48},{48,56},{1,9},{9,17},... | collective-permute-start | bytes 49160 | tf_op jit(solution)/shard_map/ppermute | solution.py:17
  176.9 8.2 %collective-permute-start.28 = (bf16[8,8,1,128]{3,2,1,0:T(2,128)(2,1)S(1)}, bf16[8,8,1,128]{3,2,1,0:T(2,128)(2,1)S(1)}, u32[]{:S(2)}, u32[]{:S(2)}) collective-permute-start(bf16[8,8,1,128]{3,2,1,0:T(2,128)(2,1)S(1)} %slice.626), channel_id=1, source_target_pairs={{1,0},{2,1},{3,2},{4,3},{5,4},{6,5},{7,6},{9,8},{10,9},{11,10},{12... | collective-permute-start | bytes 49160 | tf_op jit(solution)/shard_map/ppermute | solution.py:17
  178.9 7.1 %collective-permute-start.29 = (bf16[8,8,1,128]{3,2,1,0:T(2,128)(2,1)S(1)}, bf16[8,8,1,128]{3,2,1,0:T(2,128)(2,1)S(1)}, u32[]{:S(2)}, u32[]{:S(2)}) collective-permute-start(bf16[8,8,1,128]{3,2,1,0:T(2,128)(2,1)S(1)} %slice.628), channel_id=1, source_target_pairs={{0,1},{1,2},{2,3},{3,4},{4,5},{5,6},{6,7},{8,9},{9,10},{10,11},{11... | collective-permute-start | bytes 49160 | tf_op jit(solution)/shard_map/ppermute | solution.py:17
  193.0 13.7 %collective-permute-start.30 = (bf16[1,8,8,128]{3,2,1,0:T(8,128)(2,1)S(1)}, bf16[1,8,8,128]{3,2,1,0:T(8,128)(2,1)S(1)}, u32[]{:S(2)}, u32[]{:S(2)}) collective-permute-start(bf16[1,8,8,128]{3,2,1,0:T(8,128)(2,1)S(1)} %slice.632), channel_id=1, source_target_pairs={{64,0},{128,64},{192,128},{65,1},{129,65},{193,129},{66,2},{130,66... | collective-permute-start | bytes 49160 | tf_op jit(solution)/shard_map/ppermute | solution.py:17
  195.1 17.9 %collective-permute-start.31 = (bf16[1,8,8,128]{3,2,1,0:T(8,128)(2,1)S(1)}, bf16[1,8,8,128]{3,2,1,0:T(8,128)(2,1)S(1)}, u32[]{:S(2)}, u32[]{:S(2)}) collective-permute-start(bf16[1,8,8,128]{3,2,1,0:T(8,128)(2,1)S(1)} %slice.634), channel_id=1, source_target_pairs={{0,64},{64,128},{128,192},{1,65},{65,129},{129,193},{2,66},{66,130... | collective-permute-start | bytes 49160 | tf_op jit(solution)/shard_map/ppermute | solution.py:17
  199.1 14.0 %collective-permute-start.32 = (bf16[8,1,8,128]{3,2,1,0:T(8,128)(2,1)S(1)}, bf16[8,1,8,128]{3,2,1,0:T(8,128)(2,1)S(1)}, u32[]{:S(2)}, u32[]{:S(2)}) collective-permute-start(bf16[8,1,8,128]{3,2,1,0:T(8,128)(2,1)S(1)} %slice.638), channel_id=1, source_target_pairs={{8,0},{16,8},{24,16},{32,24},{40,32},{48,40},{56,48},{9,1},{17,9},... | collective-permute-start | bytes 49160 | tf_op jit(solution)/shard_map/ppermute | solution.py:17
  200.4 12.7 %collective-permute-start.33 = (bf16[8,1,8,128]{3,2,1,0:T(8,128)(2,1)S(1)}, bf16[8,1,8,128]{3,2,1,0:T(8,128)(2,1)S(1)}, u32[]{:S(2)}, u32[]{:S(2)}) collective-permute-start(bf16[8,1,8,128]{3,2,1,0:T(8,128)(2,1)S(1)} %slice.640), channel_id=1, source_target_pairs={{0,8},{8,16},{16,24},{24,32},{32,40},{40,48},{48,56},{1,9},{9,17},... | collective-permute-start | bytes 49160 | tf_op jit(solution)/shard_map/ppermute | solution.py:17
  204.8 8.3 %collective-permute-start.34 = (bf16[8,8,1,128]{3,2,1,0:T(2,128)(2,1)S(1)}, bf16[8,8,1,128]{3,2,1,0:T(2,128)(2,1)S(1)}, u32[]{:S(2)}, u32[]{:S(2)}) collective-permute-start(bf16[8,8,1,128]{3,2,1,0:T(2,128)(2,1)S(1)} %slice.644), channel_id=1, source_target_pairs={{1,0},{2,1},{3,2},{4,3},{5,4},{6,5},{7,6},{9,8},{10,9},{11,10},{12... | collective-permute-start | bytes 49160 | tf_op jit(solution)/shard_map/ppermute | solution.py:17
  206.7 7.0 %collective-permute-start.35 = (bf16[8,8,1,128]{3,2,1,0:T(2,128)(2,1)S(1)}, bf16[8,8,1,128]{3,2,1,0:T(2,128)(2,1)S(1)}, u32[]{:S(2)}, u32[]{:S(2)}) collective-permute-start(bf16[8,8,1,128]{3,2,1,0:T(2,128)(2,1)S(1)} %slice.646), channel_id=1, source_target_pairs={{0,1},{1,2},{2,3},{3,4},{4,5},{5,6},{6,7},{8,9},{9,10},{10,11},{11... | collective-permute-start | bytes 49160 | tf_op jit(solution)/shard_map/ppermute | solution.py:17
  (83 other events, 760.2 us)
Sparse Core Ops, SparseCore 0:
  218.8 252.5 all-reduce.1
where the time goes:
time: 482 us; the launch traced here: 480 us
  waiting for transfers between devices  277 us (57%)
  starting transfers between devices  109 us (23%)
  other arithmetic  36 us (7%)
  matrix products  24 us (5%)
  local copies, waits for them, and re-layouts  17.3 us (4%)
  between operations  16.5 us (3%)
    psum x1, waiting for transfers between devices, on_device(): combined = lax.psum(combined, ('gx', 'gy', 'gz'))  252 us
    ppermute x18, starting transfers between devices, from_behind(): lax.ppermute(value, axis, [(source, source + steps) for source in range(f...  55.5 us
    ppermute x9, starting transfers between devices, with_halo(): lax.ppermute(lax.slice_in_dim(block, block.shape[dim] - width, None, axis...  39.9 us
    ppermute x9, waiting for transfers between devices, with_halo(): lax.ppermute(lax.slice_in_dim(block, 0, width, axis=dim), axis, backward)  23.3 us
    dot_general x24, matrix products, project(): jnp.dot(operand.reshape(-1, operand.shape[-1]), table, preferred_element_...  18.7 us
    ppermute x9, starting transfers between devices, with_halo(): lax.ppermute(lax.slice_in_dim(block, 0, width, axis=dim), axis, backward)  13.5 us
    div x1, other arithmetic, on_device(): belief = product / jnp.sum(product, axis=-1, keepdims=True)  10.5 us
  transfers between devices with their start and end apart: 37, of which 13 were waited for; matrix products, arithmetic and copies ran while one was open for 2% of the time, Pallas kernels for 0%

commit v1 on v0

v1 whole, which is shorter than its diff:
```python
import math

import jax
import jax.numpy as jnp
from jax import lax
from jax.experimental import pallas as pl
from jax.experimental.pallas import tpu as pltpu
from jax.sharding import PartitionSpec as P

LABELS = 128
CELLS = 131072
AXES = ("gx", "gy", "gz")
F32 = jnp.float32
BF16 = jnp.bfloat16
MESH = pl.DeviceIdType.MESH


def take(ref, lead, axis, upper):
    if axis == 0:
        return ref[(*lead, 8 if upper else 1)]
    if axis == 1:
        rows = pl.ds(56 if upper else 0, 8)
    else:
        rows = pl.ds(7 if upper else 0, 8, stride=8)
    return ref[(*lead, pl.ds(1, 8), rows)].reshape(64, LABELS)


def put(ref, lead, axis, upper, value):
    if axis == 0:
        ref[(*lead, 8 if upper else 1)] = value
        return
    if axis == 1:
        rows = pl.ds(56 if upper else 0, 8)
    else:
        rows = pl.ds(7 if upper else 0, 8, stride=8)
    ref[(*lead, pl.ds(1, 8), rows)] = value.reshape(8, 8, LABELS)


def turn(value, steps):
    rows = value.shape[0]
    tiles = value.reshape(rows // 8, 8, LABELS)
    return pltpu.roll(tiles, steps % 8, 1).reshape(rows, LABELS)


def dot(a, b):
    return jnp.dot(a.astype(BF16), b, preferred_element_type=F32)


def dot_rows(a, b):
    return lax.dot_general(a, b, (((0,), (0,)), ((), ())), preferred_element_type=F32)


def lanes(value):
    return jnp.sum(value, axis=-1, keepdims=True)


def wide(value):
    return jnp.broadcast_to(value, (value.shape[0], LABELS))


def cavities(unary, incoming):
    xs = incoming[0] * incoming[1]
    ys = incoming[2] * incoming[3]
    zs = incoming[4] * incoming[5]
    ux = unary * xs
    no_z = ux * ys
    no_y = ux * zs
    no_x = unary * ys * zs
    rest = (no_x, no_x, no_y, no_y, no_z, no_z)
    return [rest[d] * incoming[d] for d in range(6)], no_z * zs


def kernel(
    q_hbm, pot_hbm, bg_hbm, ug_hbm, pg_hbm,
    q, pot, bg, table, table_t, unary, inc, cav, cav16, inv_s, inv_t, inv_s1, inv_t1,
    log_grad, parts, whole, sgrad16, pair, ug, out_face, in_face, ghost_u, ghost_is, ghost_it,
    part1, part2, sum16, sums, final,
    in_sem, out_sem, face_ss, face_rs, s1_ss, s1_rs, s2_ss, s2_rs, s3_ss, s3_rs,
):
    gx, gy, gz = (lax.axis_index(a) for a in AXES)
    nx, ny, nz = (lax.axis_size(a) for a in AXES)

    def beside(axis, step):
        at = [gx, gy, gz]
        size = (nx, ny, nz)[axis]
        at[axis] = lax.rem(at[axis] + step + size, size)
        return tuple(at)

    neighbour = [beside(d // 2, 1 - 2 * (d % 2)) for d in range(6)]
    at_low = (gx == 0, gy == 0, gz == 0)
    at_high = (gx == nx - 1, gy == ny - 1, gz == nz - 1)
    outside = [(at_high if d % 2 else at_low)[d // 2] for d in range(6)]

    core = lax.rem(gz, 2)
    first_id = gx * 2 + core
    firsts = nx * 2
    second_id = gy * (nz // 2) + gz // 2
    seconds = ny * (nz // 2)

    def first_peer(k):
        j = lax.rem(first_id + k, firsts)
        return (j // 2, gy, gz - core + lax.rem(j, 2))

    def second_peer(k):
        j = lax.rem(second_id + k, seconds)
        return (gx, j // (nz // 2), lax.rem(j, nz // 2) * 2 + core)

    loads = [
        pltpu.make_async_copy(q_hbm, q, in_sem.at[0]),
        pltpu.make_async_copy(pot_hbm, pot, in_sem.at[1]),
        pltpu.make_async_copy(bg_hbm, bg, in_sem.at[2]),
    ]
    for load in loads:
        load.start()
    barrier = pltpu.get_barrier_semaphore()
    met = 0
    for place in neighbour:
        pl.semaphore_signal(barrier, inc=1, device_id=place, device_id_type=MESH)
        met += 1
    for k in range(1, firsts):
        pl.semaphore_signal(barrier, inc=1, device_id=first_peer(k), device_id_type=MESH)
        met += 1
    for k in range(1, seconds):
        pl.semaphore_signal(barrier, inc=1, device_id=second_peer(k), device_id_type=MESH)
        met += 1

    started = []

    def send(stage, slot, target, value):
        out_face[stage, slot] = value.astype(BF16)
        copy = pltpu.make_async_remote_copy(
            src_ref=out_face.at[stage, slot],
            dst_ref=in_face.at[stage, slot],
            send_sem=face_ss.at[stage, slot],
            recv_sem=face_rs.at[stage, slot],
            device_id=target,
            device_id_type=MESH,
        )
        copy.start()
        started.append(copy)
        return copy

    loads[0].wait()

    def factors(x, _):
        unary[x + 1] = q[x].astype(F32)
        return 0

    lax.fori_loop(0, 8, factors, 0)
    pl.semaphore_wait(barrier, met)
    copies = [send(0, d, neighbour[d], take(unary, (), d // 2, d % 2 == 0)) for d in range(6)]

    loads[1].wait()
    factor = jnp.exp(pot[...].astype(F32) / 64.0)
    table[...] = factor.astype(BF16)
    table_t[...] = factor.T.astype(BF16)

    def push(t, d, x, message):
        if d == 0:
            inc[t, d, x + 2] = message
        elif d == 1:
            inc[t, d, x] = message
        elif d == 2:
            inc[t, d, x + 1, pl.ds(8, 56)] = message[:56]
        elif d == 3:
            inc[t, d, x + 1, pl.ds(0, 56)] = message[8:]
        elif d == 4:
            inc[t, d, x + 1] = turn(message, 1)
        else:
            inc[t, d, x + 1] = turn(message, -1)

    def first_messages(x, _):
        value = jnp.exp(unary[x + 1] / 32.0)
        unary[x + 1] = value
        scores = dot(value, table[...])
        inv_total = 1.0 / lanes(scores)
        inv_s1[x + 1] = 1.0 / scores
        inv_t1[x + 1] = wide(inv_total)
        message = scores * (LABELS * inv_total)
        for d in range(6):
            push(0, d, x, message)
        return 0

    lax.fori_loop(0, 8, first_messages, 0)

    for copy in copies:
        copy.wait_recv()
    value = jnp.exp(in_face[0].astype(F32).reshape(384, LABELS) / 32.0)
    scores = dot(value, table[...])
    inv_total = 1.0 / lanes(scores)
    ghost_u[...] = value.astype(BF16)
    ghost_is[...] = 1.0 / scores
    ghost_it[...] = wide(inv_total)
    message = scores * (LABELS * inv_total)
    for d in range(6):
        face = message[d * 64 : d * 64 + 64]
        put(inc, (0, d), d // 2, d % 2 == 1, jnp.where(outside[d], 1.0, face))

    for t in (1, 2):
        faces = []
        for d in range(6):
            value = take(unary, (), d // 2, d % 2 == 0)
            for e in range(6):
                if e != d ^ 1:
                    value = value * take(inc, (t - 1, e), d // 2, d % 2 == 0)
            faces.append(value.astype(BF16))
        scores = dot(jnp.concatenate(faces, axis=0), table[...])
        message = scores * (LABELS / lanes(scores))
        copies = [send(t, d, neighbour[d], message[d * 64 : d * 64 + 64]) for d in range(6)]

        def messages(x, _, t=t):
            values, _ = cavities(unary[x + 1], [inc[t - 1, d, x + 1] for d in range(6)])
            for d in range(6):
                rounded = values[d].astype(BF16)
                cav[t - 1, d, x + 1] = values[d]
                cav16[t - 1, d, x] = rounded
                scores = dot(rounded, table[...])
                inv_total = 1.0 / lanes(scores)
                inv_s[t - 1, d, x + 1] = 1.0 / scores
                inv_t[t - 1, d, x + 1] = wide(inv_total)
                push(t, d, x, scores * (LABELS * inv_total))
            return 0

        lax.fori_loop(0, 8, messages, 0)
        for copy in copies:
            copy.wait_recv()
        for d in range(6):
            face = in_face[t, d].astype(F32)
            put(inc, (t, d), d // 2, d % 2 == 1, jnp.where(outside[d], 1.0, face))

    loads[2].wait()
    empty = jnp.zeros((64, LABELS), F32)
    for x in (0, 9):
        log_grad[x] = empty
        for t in range(2):
            whole[t, x] = empty
            for d in range(6):
                parts[t, d, x] = empty

    def beliefs(x, _):
        product = unary[x + 1]
        for d in range(6):
            product = product * inc[2, d, x + 1]
        target = bg[x].astype(F32)
        log_grad[x + 1] = target - product * (lanes(target) / lanes(product))
        return 0

    lax.fori_loop(0, 8, beliefs, 0)
    copies = [send(3, d, neighbour[d ^ 1], take(log_grad, (), d // 2, d % 2 == 1)) for d in range(6)]

    place = lax.rem(lax.broadcasted_iota(jnp.int32, (64, LABELS), 0), 8)
    border = jnp.zeros((8, LABELS), F32)

    def arrived(read, d, x):
        if d == 0:
            return read(d, x + 2)
        if d == 1:
            return read(d, x)
        if d == 2:
            return jnp.concatenate([read(d, x + 1)[8:], border], axis=0)
        if d == 3:
            return jnp.concatenate([border, read(d, x + 1)[:56]], axis=0)
        if d == 4:
            return jnp.where(place == 7, 0.0, turn(read(d, x + 1), -1))
        return jnp.where(place == 0, 0.0, turn(read(d, x + 1), 1))

    def last_grads(d, x):
        return log_grad[x]

    def grads_of(t):
        return lambda d, x: whole[t, x] - parts[t, d ^ 1, x]

    pair[...] = jnp.zeros_like(pair)

    for t in (1, 0):
        read = last_grads if t == 1 else grads_of(1)

        def backward(x, _, t=t, read=read):
            total = None
            for d in range(6):
                grad = arrived(read, d, x)
                score_grad = grad * inv_s[t, d, x + 1] - lanes(grad) * inv_t[t, d, x + 1]
                rounded = score_grad.astype(BF16)
                sgrad16[d, x] = rounded
                part = dot(rounded, table_t[...]) * cav[t, d, x + 1]
                parts[t, d, x + 1] = part
                total = part if total is None else total + part
            whole[t, x + 1] = total
            return 0

        lax.fori_loop(0, 8, backward, 0)

        def pair_terms(d, _, t=t):
            pair[...] += dot_rows(
                cav16[t, d].reshape(512, LABELS), sgrad16[d].reshape(512, LABELS)
            )
            return 0

        lax.fori_loop(0, 6, pair_terms, 0)
        for copy in copies:
            copy.wait_recv()
        rounded, factors_at = [], []
        for d in range(6):
            upper = d % 2 == 0
            grad = jnp.where(outside[d ^ 1], 0.0, in_face[4 - t, d].astype(F32))
            score_grad = grad * take(inv_s, (t, d), d // 2, upper)
            score_grad -= lanes(grad) * take(inv_t, (t, d), d // 2, upper)
            rounded.append(score_grad.astype(BF16))
            factors_at.append(take(cav, (t, d), d // 2, upper))
        rounded = jnp.concatenate(rounded, axis=0)
        back = dot(rounded, table_t[...])
        for d in range(6):
            upper = d % 2 == 0
            part = back[d * 64 : d * 64 + 64] * factors_at[d]
            put(parts, (t, d), d // 2, upper, part)
            put(whole, (t,), d // 2, upper, take(whole, (t,), d // 2, upper) + part)
        copies = []
        edge = []
        for d in range(6):
            upper = d % 2 == 1
            grad = take(whole, (t,), d // 2, upper) - take(parts, (t, d ^ 1), d // 2, upper)
            copies.append(send(5 - t, d, neighbour[d ^ 1], grad))
            edge.append(grad)
        at = jnp.concatenate(factors_at, axis=0).astype(BF16)
        pair[...] += dot_rows(at, rounded)

    read = grads_of(0)

    def first_grads(x, _):
        grad = arrived(read, 0, x)
        for d in range(1, 6):
            grad += arrived(read, d, x)
        log_sum = grad * inv_s1[x + 1] - lanes(grad) * inv_t1[x + 1]
        rounded = log_sum.astype(BF16)
        sgrad16[0, x] = rounded
        back = dot(rounded, table_t[...]) * unary[x + 1]
        ug[x + 1] = log_grad[x + 1] + whole[1, x + 1] + whole[0, x + 1] + back
        cav16[0, 0, x] = unary[x + 1].astype(BF16)
        return 0

    lax.fori_loop(0, 8, first_grads, 0)
    pair[...] += dot_rows(cav16[0, 0].reshape(512, LABELS), sgrad16[0].reshape(512, LABELS))
    grad = jnp.concatenate([jnp.where(outside[d], 0.0, edge[d]) for d in range(6)], axis=0)
    score_grad = grad * ghost_is[...] - lanes(grad) * ghost_it[...]
    pair[...] += dot_rows(ghost_u[...], score_grad.astype(BF16))

    def copy_to(src, dst, ss, rs, target):
        copy = pltpu.make_async_remote_copy(
            src_ref=src, dst_ref=dst, send_sem=ss, recv_sem=rs, device_id=target, device_id_type=MESH
        )
        copy.start()
        started.append(copy)
        return copy

    height = LABELS // firsts

    def rows_of(j):
        return pl.ds(pl.multiple_of(j * height, height), height)

    sends = [
        copy_to(
            pair.at[rows_of(lax.rem(first_id + k, firsts))], part1.at[k - 1],
            s1_ss.at[k - 1], s1_rs.at[k - 1], first_peer(k),
        )
        for k in range(1, firsts)
    ]

    for copy in copies:
        copy.wait_recv()
    rounded = []
    for d in range(6):
        upper = d % 2 == 0
        grad = jnp.where(outside[d ^ 1], 0.0, in_face[5, d].astype(F32))
        score_grad = grad * take(inv_s1, (), d // 2, upper)
        score_grad -= lanes(grad) * take(inv_t1, (), d // 2, upper)
        rounded.append(score_grad.astype(BF16))
    back = dot(jnp.concatenate(rounded, axis=0), table_t[...])
    for d in range(6):
        upper = d % 2 == 0
        part = back[d * 64 : d * 64 + 64] * take(unary, (), d // 2, upper)
        put(ug, (), d // 2, upper, take(ug, (), d // 2, upper) + part)
    store = pltpu.make_async_copy(ug.at[pl.ds(1, 8)], ug_hbm, out_sem.at[0])
    store.start()

    for copy in sends:
        copy.wait_recv()
    mine = pair[rows_of(first_id)]
    for k in range(1, firsts):
        mine += part1[k - 1]
    sums[...] = mine
    sum16[...] = mine.astype(BF16)
    sends = [
        copy_to(sum16, part2.at[k - 1], s2_ss.at[k - 1], s2_rs.at[k - 1], second_peer(k))
        for k in range(1, seconds)
    ]
    for copy in sends:
        copy.wait_recv()
    mine = sums[...]
    for k in range(1, seconds):
        mine += part2[k - 1].astype(F32)
    final[rows_of(first_id)] = mine
    here = final.at[rows_of(first_id)]
    sends = [
        copy_to(here, here, s3_ss.at[k - 1], s3_rs.at[k - 1], first_peer(k))
        for k in range(1, firsts)
    ]
    for copy in sends:
        copy.wait_recv()
    factor = jnp.exp(pot[...].astype(F32) / 64.0)
    for copy in started:
        copy.wait_send()
    pair[...] = factor * final[...] * (LABELS / math.sqrt(CELLS))
    store2 = pltpu.make_async_copy(pair, pg_hbm, out_sem.at[1])
    store2.start()
    store.wait()
    store2.wait()


def on_device(unary_q, potential_q, belief_grad):
    slabs = (8, 64, LABELS)
    padded = (10, 64, LABELS)
    firsts = lax.axis_size("gx") * 2
    seconds = lax.axis_size("gy") * (lax.axis_size("gz") // 2)
    height = LABELS // firsts
    vmem, dma = pltpu.VMEM, pltpu.SemaphoreType.DMA
    any_space = pl.BlockSpec(memory_space=pl.ANY)
    unary_grad, potential_grad = pl.pallas_call(
        kernel,
        out_shape=(
            jax.ShapeDtypeStruct(slabs, F32),
            jax.ShapeDtypeStruct((LABELS, LABELS), F32),
        ),
        in_specs=[any_space] * 3,
        out_specs=(any_space, any_space),
        scratch_shapes=[
            vmem(slabs, jnp.int32),
            vmem((LABELS, LABELS), jnp.int32),
            vmem(slabs, BF16),
            vmem((LABELS, LABELS), BF16),
            vmem((LABELS, LABELS), BF16),
            vmem(padded, F32),
            vmem((3, 6, *padded), F32),
            vmem((2, 6, *padded), F32),
            vmem((2, 6, *slabs), BF16),
            vmem((2, 6, *padded), F32),
            vmem((2, 6, *padded), F32),
            vmem(padded, F32),
            vmem(padded, F32),
            vmem(padded, F32),
            vmem((2, 6, *padded), F32),
            vmem((2, *padded), F32),
            vmem((6, *slabs), BF16),
            vmem((LABELS, LABELS), F32),
            vmem(padded, F32),
            vmem((6, 6, 64, LABELS), BF16),
            vmem((6, 6, 64, LABELS), BF16),
            vmem((384, LABELS), BF16),
            vmem((384, LABELS), F32),
            vmem((384, LABELS), F32),
            vmem((firsts - 1, height, LABELS), F32),
            vmem((seconds - 1, height, LABELS), BF16),
            vmem((height, LABELS), BF16),
            vmem((height, LABELS), F32),
            vmem((LABELS, LABELS), F32),
            dma((3,)),
            dma((2,)),
            dma((6, 6)),
            dma((6, 6)),
            dma((firsts - 1,)),
            dma((firsts - 1,)),
            dma((seconds - 1,)),
            dma((seconds - 1,)),
            dma((firsts - 1,)),
            dma((firsts - 1,)),
        ],
        compiler_params=pltpu.CompilerParams(
            collective_id=0, has_side_effects=True, vmem_limit_bytes=48 * 2**20
        ),
    )(unary_q.reshape(slabs), potential_q, belief_grad.reshape(slabs))
    return unary_grad.reshape(unary_q.shape), potential_grad


def solution(mesh):
    return jax.shard_map(
        on_device,
        mesh=mesh,
        in_specs=(P("gx", "gy", "gz", None), P(), P("gx", "gy", "gz", None)),
        out_specs=(P("gx", "gy", "gz", None), P()),
        check_vma=False,
    )
```

time: 482 us -> 55.1 us (0.11)
  waiting for transfers between devices: 277 us -> 0 us
  starting transfers between devices: 109 us -> 0 us
  Pallas kernels: 0 us -> 50.2 us
  other arithmetic: 36 us -> 0 us
  matrix products: 24 us -> 0 us
  between operations: 16.5 us -> 0.65 us
  local copies, waits for them, and re-layouts: 17.3 us -> 4.02 us
    psum x1 -> x0, waiting for transfers between devices: 252 us -> none  [on_device(): combined = lax.psum(combined, ('gx', 'gy', 'gz'))]
    ppermute x36 -> x0, starting transfers between devices: 109 us -> none  [the longest x18 55.5 us: from_behind(): lax.ppermute(value, axis, [(source, source + steps) for source in range(f...]
    pallas_call x0 -> x1, Pallas kernels: none -> 50.2 us  [on_device(): pl.pallas_call(kernel, out_shape=(jax.ShapeDtypeStruct(slabs, F32), jax.S...]
    ppermute x36 -> x0, waiting for transfers between devices: 25.2 us -> none  [the longest x9 23.3 us: with_halo(): lax.ppermute(lax.slice_in_dim(block, 0, width, axis=dim), axis, backward)]
    dot_general x27 -> x0, matrix products: 24 us -> none  [the longest x24 18.7 us: project(): jnp.dot(operand.reshape(-1, operand.shape[-1]), table, preferred_element_...]
    convert_element_type x20 -> x0, other arithmetic: 11.8 us -> none  [the longest x2 4.51 us: on_device(): score_grad = (labels / totals * (back_grad - weight)).astype(jnp.bfloat16)]
    div x5 -> x0, other arithmetic: 11.2 us -> none  [the longest x1 10.5 us: on_device(): belief = product / jnp.sum(product, axis=-1, keepdims=True)]
    div x23 -> x0, local copies, waits for them, and re-layouts: 9.39 us -> none  [the longest x18 8.79 us: pass_products(): labels * scores / totals]
  transfers between devices with their start and end apart: 37 -> 0, of which waited for: 13 -> 0; matrix products, arithmetic and copies ran while one was open for 2% -> 0% of each run, Pallas kernels for 0% -> 0%
where the time goes in v1:
time: 55.1 us; the launch traced here: 54.9 us
  Pallas kernels  50.2 us (91%)
  local copies, waits for them, and re-layouts  4.02 us (7%)
  between operations  0.65 us (1%)
    pallas_call x1, Pallas kernels, on_device(): pl.pallas_call(kernel, out_shape=(jax.ShapeDtypeStruct(slabs, F32), jax.S...  50.2 us
    unnamed x8, local copies, waits for them, and re-layouts  4.02 us

profile of v1, /device:TPU:1, one launch (start us, length us, event | category | flops | bytes accessed | tf_op | source)
XLA Modules:
  0.0 54.9 jit_solution(17704617029196800680)
XLA Ops:
  0.6 0.0 copy-start
  0.6 0.9 %copy-done = s32[8,8,8,128]{3,2,1,0:T(8,128)S(1)} copy-done((s32[8,8,8,128]{3,2,1,0:T(8,128)S(1)}, s32[8,8,8,128]{3,2,1,0:T(8,128)}, u32[]{:S(2)}) %copy-start) | copy-done | bytes 262168
  1.6 0.0 copy-start.1
  1.6 0.9 %copy-done.1 = bf16[8,8,8,128]{3,2,1,0:T(8,128)(2,1)S(1)} copy-done((bf16[8,8,8,128]{3,2,1,0:T(8,128)(2,1)S(1)}, bf16[8,8,8,128]{3,2,1,0:T(8,128)(2,1)}, u32[]{:S(2)}) %copy-start.1) | copy-done | bytes 131096
  2.5 0.0 copy-start.2
  2.5 0.8 %copy-done.2 = s32[128,128]{1,0:T(8,128)S(1)} copy-done((s32[128,128]{1,0:T(8,128)S(1)}, s32[128,128]{1,0:T(8,128)}, u32[]{:S(2)}) %copy-start.2) | copy-done | bytes 65560
  3.3 50.2 %shard_map.50 = (f32[8,64,128]{2,1,0:T(8,128)S(1)}, f32[128,128]{1,0:T(8,128)S(1)}) custom-call(s32[8,64,128]{2,1,0:T(8,128)S(1)} %bitcast.3, s32[128,128]{1,0:T(8,128)S(1)} %copy-done.2, bf16[8,64,128]{2,1,0:T(8,128)(2,1)S(1)} %bitcast.5), custom_call_target="tpu_custom_call" | custom-call | tf_op jit(solution)/shard_map/pallas_call | solution.py:427
  53.6 0.7 %copy.7 = f32[8,8,8,128]{3,2,1,0:T(8,128)} copy(f32[8,8,8,128]{3,2,1,0:T(8,128)S(1)} %bitcast.4) | data formatting | bytes 524288
  54.3 0.6 %copy.8 = f32[128,128]{1,0:T(8,128)} copy(f32[128,128]{1,0:T(8,128)S(1)} %get-tuple-element.9) | data formatting | bytes 131072
Async XLA Ops:
  0.6 1.0 %copy-start = (s32[8,8,8,128]{3,2,1,0:T(8,128)S(1)}, s32[8,8,8,128]{3,2,1,0:T(8,128)}, u32[]{:S(2)}) copy-start(s32[8,8,8,128]{3,2,1,0:T(8,128)} %param.3) | copy-start | bytes 786436
  1.6 0.9 %copy-start.1 = (bf16[8,8,8,128]{3,2,1,0:T(8,128)(2,1)S(1)}, bf16[8,8,8,128]{3,2,1,0:T(8,128)(2,1)}, u32[]{:S(2)}) copy-start(bf16[8,8,8,128]{3,2,1,0:T(8,128)(2,1)} %param.5) | copy-start | bytes 393220
  2.5 0.8 %copy-start.2 = (s32[128,128]{1,0:T(8,128)S(1)}, s32[128,128]{1,0:T(8,128)}, u32[]{:S(2)}) copy-start(s32[128,128]{1,0:T(8,128)} %pot_hbm.1) | copy-start | bytes 196612

commit v2 on v1

--- a/solution.py
+++ b/solution.py
@@ -71,10 +71,10 @@
 
 
 def kernel(
-    q_hbm, pot_hbm, bg_hbm, ug_hbm, pg_hbm,
+    q_hbm, pot_hbm, bg_hbm, ug_out, pg_out,
     q, pot, bg, table, table_t, unary, inc, cav, cav16, inv_s, inv_t, inv_s1, inv_t1,
     log_grad, parts, whole, sgrad16, pair, ug, out_face, in_face, ghost_u, ghost_is, ghost_it,
-    part1, part2, sum16, sums, final,
+    part1, part2, final,
     in_sem, out_sem, face_ss, face_rs, s1_ss, s1_rs, s2_ss, s2_rs, s3_ss, s3_rs,
 ):
     gx, gy, gz = (lax.axis_index(a) for a in AXES)
@@ -146,7 +146,7 @@
         unary[x + 1] = q[x].astype(F32)
         return 0
 
-    lax.fori_loop(0, 8, factors, 0)
+    lax.fori_loop(0, 8, factors, 0, unroll=True)
     pl.semaphore_wait(barrier, met)
     copies = [send(0, d, neighbour[d], take(unary, (), d // 2, d % 2 == 0)) for d in range(6)]
 
@@ -181,7 +181,7 @@
             push(0, d, x, message)
         return 0
 
-    lax.fori_loop(0, 8, first_messages, 0)
+    lax.fori_loop(0, 8, first_messages, 0, unroll=True)
 
     for copy in copies:
         copy.wait_recv()
@@ -221,7 +221,7 @@
                 push(t, d, x, scores * (LABELS * inv_total))
             return 0
 
-        lax.fori_loop(0, 8, messages, 0)
+        lax.fori_loop(0, 8, messages, 0, unroll=True)
         for copy in copies:
             copy.wait_recv()
         for d in range(6):
@@ -245,7 +245,7 @@
         log_grad[x + 1] = target - product * (lanes(target) / lanes(product))
         return 0
 
-    lax.fori_loop(0, 8, beliefs, 0)
+    lax.fori_loop(0, 8, beliefs, 0, unroll=True)
     copies = [send(3, d, neighbour[d ^ 1], take(log_grad, (), d // 2, d % 2 == 1)) for d in range(6)]
 
     place = lax.rem(lax.broadcasted_iota(jnp.int32, (64, LABELS), 0), 8)
@@ -288,7 +288,7 @@
             whole[t, x + 1] = total
             return 0
 
-        lax.fori_loop(0, 8, backward, 0)
+        lax.fori_loop(0, 8, backward, 0, unroll=True)
 
         def pair_terms(d, _, t=t):
             pair[...] += dot_rows(
@@ -296,7 +296,7 @@
             )
             return 0
 
-        lax.fori_loop(0, 6, pair_terms, 0)
+        lax.fori_loop(0, 6, pair_terms, 0, unroll=True)
         for copy in copies:
             copy.wait_recv()
         rounded, factors_at = [], []
@@ -338,7 +338,7 @@
         cav16[0, 0, x] = unary[x + 1].astype(BF16)
         return 0
 
-    lax.fori_loop(0, 8, first_grads, 0)
+    lax.fori_loop(0, 8, first_grads, 0, unroll=True)
     pair[...] += dot_rows(cav16[0, 0].reshape(512, LABELS), sgrad16[0].reshape(512, LABELS))
     grad = jnp.concatenate([jnp.where(outside[d], 0.0, edge[d]) for d in range(6)], axis=0)
     score_grad = grad * ghost_is[...] - lanes(grad) * ghost_it[...]
@@ -379,7 +379,7 @@
         upper = d % 2 == 0
         part = back[d * 64 : d * 64 + 64] * take(unary, (), d // 2, upper)
         put(ug, (), d // 2, upper, take(ug, (), d // 2, upper) + part)
-    store = pltpu.make_async_copy(ug.at[pl.ds(1, 8)], ug_hbm, out_sem.at[0])
+    store = pltpu.make_async_copy(ug.at[pl.ds(1, 8)], ug_out, out_sem.at[0])
     store.start()
 
     for copy in sends:
@@ -387,18 +387,15 @@
     mine = pair[rows_of(first_id)]
     for k in range(1, firsts):
         mine += part1[k - 1]
-    sums[...] = mine
-    sum16[...] = mine.astype(BF16)
+    part2[second_id] = mine.astype(BF16)
+    own = part2.at[second_id]
     sends = [
-        copy_to(sum16, part2.at[k - 1], s2_ss.at[k - 1], s2_rs.at[k - 1], second_peer(k))
+        copy_to(own, own, s2_ss.at[k - 1], s2_rs.at[k - 1], second_peer(k))
         for k in range(1, seconds)
     ]
     for copy in sends:
         copy.wait_recv()
-    mine = sums[...]
-    for k in range(1, seconds):
-        mine += part2[k - 1].astype(F32)
-    final[rows_of(first_id)] = mine
+    final[rows_of(first_id)] = jnp.sum(part2[...].astype(F32), axis=0)
     here = final.at[rows_of(first_id)]
     sends = [
         copy_to(here, here, s3_ss.at[k - 1], s3_rs.at[k - 1], first_peer(k))
@@ -410,7 +407,7 @@
     for copy in started:
         copy.wait_send()
     pair[...] = factor * final[...] * (LABELS / math.sqrt(CELLS))
-    store2 = pltpu.make_async_copy(pair, pg_hbm, out_sem.at[1])
+    store2 = pltpu.make_async_copy(pair, pg_out, out_sem.at[1])
     store2.start()
     store.wait()
     store2.wait()
@@ -423,15 +420,14 @@
     seconds = lax.axis_size("gy") * (lax.axis_size("gz") // 2)
     height = LABELS // firsts
     vmem, dma = pltpu.VMEM, pltpu.SemaphoreType.DMA
-    any_space = pl.BlockSpec(memory_space=pl.ANY)
     unary_grad, potential_grad = pl.pallas_call(
         kernel,
         out_shape=(
             jax.ShapeDtypeStruct(slabs, F32),
             jax.ShapeDtypeStruct((LABELS, LABELS), F32),
         ),
-        in_specs=[any_space] * 3,
-        out_specs=(any_space, any_space),
+        in_specs=[pl.BlockSpec(memory_space=pltpu.HBM)] * 3,
+        out_specs=(pl.BlockSpec(memory_space=pltpu.HBM),) * 2,
         scratch_shapes=[
             vmem(slabs, jnp.int32),
             vmem((LABELS, LABELS), jnp.int32),
@@ -458,9 +454,7 @@
             vmem((384, LABELS), F32),
             vmem((384, LABELS), F32),
             vmem((firsts - 1, height, LABELS), F32),
-            vmem((seconds - 1, height, LABELS), BF16),
-            vmem((height, LABELS), BF16),
-            vmem((height, LABELS), F32),
+            vmem((seconds, height, LABELS), BF16),
             vmem((LABELS, LABELS), F32),
             dma((3,)),
             dma((2,)),
@@ -474,7 +468,7 @@
             dma((firsts - 1,)),
         ],
         compiler_params=pltpu.CompilerParams(
-            collective_id=0, has_side_effects=True, vmem_limit_bytes=48 * 2**20
+            collective_id=0, has_side_effects=True, vmem_limit_bytes=60 * 2**20
         ),
     )(unary_q.reshape(slabs), potential_q, belief_grad.reshape(slabs))
     return unary_grad.reshape(unary_q.shape), potential_grad

time: 55.1 us -> 51.7 us (0.938)
  local copies, waits for them, and re-layouts: 4.02 us -> 2.34 us
  Pallas kernels: 50.2 us -> 48.6 us
    unnamed x8 -> x4, local copies, waits for them, and re-layouts: 4.02 us -> 2.34 us
    pallas_call x1, Pallas kernels: 50.2 us -> 48.6 us  [on_device(): pl.pallas_call(kernel, out_shape=(jax.ShapeDtypeStruct(slabs, F32), jax.S...]
where the time goes in v2:
time: 51.7 us; the launch traced here: 51.6 us
  Pallas kernels  48.6 us (94%)
  local copies, waits for them, and re-layouts  2.34 us (5%)
  between operations  0.65 us (1%)
    pallas_call x1, Pallas kernels, on_device(): pl.pallas_call(kernel, out_shape=(jax.ShapeDtypeStruct(slabs, F32), jax.S...  48.6 us
    unnamed x4, local copies, waits for them, and re-layouts  2.34 us

profile of v2, /device:TPU:1, one launch (start us, length us, event | category | flops | bytes accessed | tf_op | source)
XLA Modules:
  0.0 51.6 jit_solution(17257385830741589001)
XLA Ops:
  0.6 48.6 %shard_map.50 = (f32[8,64,128]{2,1,0:T(8,128)}, f32[128,128]{1,0:T(8,128)}) custom-call(s32[8,64,128]{2,1,0:T(8,128)} %bitcast.3, s32[128,128]{1,0:T(8,128)} %pot_hbm.1, bf16[8,64,128]{2,1,0:T(8,128)(2,1)} %bitcast.5), custom_call_target="tpu_custom_call" | custom-call | tf_op jit(solution)/shard_map/pallas_call | solution.py:423
  49.3 0.0 copy-start
  49.3 1.7 %copy.7 = f32[8,8,8,128]{3,2,1,0:T(8,128)} copy(f32[8,8,8,128]{3,2,1,0:T(8,128)} %bitcast.4) | data formatting | bytes 524288
  51.0 0.0 copy-done
  51.0 0.6 %copy.8 = f32[128,128]{1,0:T(8,128)} copy(f32[128,128]{1,0:T(8,128)S(1)} %copy-done) | data formatting | bytes 131072
Async XLA Ops:
  49.3 1.7 %copy-start = (f32[128,128]{1,0:T(8,128)S(1)}, f32[128,128]{1,0:T(8,128)}, u32[]{:S(2)}) copy-start(f32[128,128]{1,0:T(8,128)} %get-tuple-element.9) | copy-start | bytes 196612

commit v3 on v2

--- a/solution.py
+++ b/solution.py
@@ -13,6 +13,8 @@
 F32 = jnp.float32
 BF16 = jnp.bfloat16
 MESH = pl.DeviceIdType.MESH
+EDGES = [(d, e) for d in range(6) for e in range(d + 1, 6) if d // 2 != e // 2]
+GHOSTS = 6 * 128 + len(EDGES) * 8
 
 
 def take(ref, lead, axis, upper):
@@ -23,6 +25,20 @@
     else:
         rows = pl.ds(7 if upper else 0, 8, stride=8)
     return ref[(*lead, pl.ds(1, 8), rows)].reshape(64, LABELS)
+
+
+def layer(ref, axis, index):
+    if axis == 0:
+        return ref[index + 1]
+    if axis == 1:
+        rows = pl.ds(index * 8, 8)
+    else:
+        rows = pl.ds(index, 8, stride=8)
+    return ref[pl.ds(1, 8), rows].reshape(64, LABELS)
+
+
+def edge_at(d, e):
+    return EDGES.index((d, e) if d < e else (e, d))
 
 
 def put(ref, lead, axis, upper, value):
@@ -73,9 +89,10 @@
 def kernel(
     q_hbm, pot_hbm, bg_hbm, ug_out, pg_out,
     q, pot, bg, table, table_t, unary, inc, cav, cav16, inv_s, inv_t, inv_s1, inv_t1,
-    log_grad, parts, whole, sgrad16, pair, ug, out_face, in_face, ghost_u, ghost_is, ghost_it,
+    log_grad, parts, whole, sgrad16, pair, ug, out_face, in_face, ghost_u, ghost_is, ghost_it, ghost_m, ghost_g,
+    ghost_c, ghost_is2, ghost_it2, side, line_out, line_in, halo_out, halo_in,
     part1, part2, final,
-    in_sem, out_sem, face_ss, face_rs, s1_ss, s1_rs, s2_ss, s2_rs, s3_ss, s3_rs,
+    in_sem, out_sem, face_ss, face_rs, halo_ss, halo_rs, line_ss, line_rs, s1_ss, s1_rs, s2_ss, s2_rs, s3_ss, s3_rs,
 ):
     gx, gy, gz = (lax.axis_index(a) for a in AXES)
     nx, ny, nz = (lax.axis_size(a) for a in AXES)
@@ -87,6 +104,11 @@
         return tuple(at)
 
     neighbour = [beside(d // 2, 1 - 2 * (d % 2)) for d in range(6)]
+    across = []
+    for d, e in EDGES:
+        at = list(neighbour[d])
+        at[e // 2] = neighbour[e][e // 2]
+        across.append(tuple(at))
     at_low = (gx == 0, gy == 0, gz == 0)
     at_high = (gx == nx - 1, gy == ny - 1, gz == nz - 1)
     outside = [(at_high if d % 2 else at_low)[d // 2] for d in range(6)]
@@ -114,7 +136,7 @@
         load.start()
     barrier = pltpu.get_barrier_semaphore()
     met = 0
-    for place in neighbour:
+    for place in neighbour + across:
         pl.semaphore_signal(barrier, inc=1, device_id=place, device_id_type=MESH)
         met += 1
     for k in range(1, firsts):
@@ -148,7 +170,32 @@
 
     lax.fori_loop(0, 8, factors, 0, unroll=True)
     pl.semaphore_wait(barrier, met)
-    copies = [send(0, d, neighbour[d], take(unary, (), d // 2, d % 2 == 0)) for d in range(6)]
+    copies = []
+
+    def send_from(src, dst, ss, rs, target):
+        copy = pltpu.make_async_remote_copy(
+            src_ref=src, dst_ref=dst, send_sem=ss, recv_sem=rs, device_id=target, device_id_type=MESH
+        )
+        copy.start()
+        started.append(copy)
+        return copy
+
+    for k, (d, e) in enumerate(EDGES):
+        near = [7 if f % 2 == 0 else 0 for f in (d, e)]
+        if (d // 2, e // 2) == (0, 1):
+            line_out[k] = unary[near[0] + 1, pl.ds(near[1] * 8, 8)]
+        elif (d // 2, e // 2) == (0, 2):
+            line_out[k] = unary[near[0] + 1, pl.ds(near[1], 8, stride=8)]
+        else:
+            for x in range(8):
+                row = pl.ds(near[0] * 8 + near[1], 1)
+                line_out[k, pl.ds(x, 1)] = unary[x + 1, row]
+        copies.append(send_from(line_out.at[k], line_in.at[k], line_ss.at[k], line_rs.at[k], across[k]))
+    for d in range(6):
+        near, behind = (7, 6) if d % 2 == 0 else (0, 1)
+        halo_out[d, pl.ds(0, 64)] = layer(unary, d // 2, near).astype(BF16)
+        halo_out[d, pl.ds(64, 64)] = layer(unary, d // 2, behind).astype(BF16)
+        copies.append(send_from(halo_out.at[d], halo_in.at[d], halo_ss.at[d], halo_rs.at[d], neighbour[d]))
 
     loads[1].wait()
     factor = jnp.exp(pot[...].astype(F32) / 64.0)
@@ -185,28 +232,56 @@
 
     for copy in copies:
         copy.wait_recv()
-    value = jnp.exp(in_face[0].astype(F32).reshape(384, LABELS) / 32.0)
+    scores_in = jnp.concatenate(
+        [halo_in[...].astype(F32).reshape(768, LABELS), line_in[...].reshape(96, LABELS)], axis=0
+    )
+    value = jnp.exp(scores_in / 32.0)
     scores = dot(value, table[...])
     inv_total = 1.0 / lanes(scores)
-    ghost_u[...] = value.astype(BF16)
+    ghost_u[...] = value
     ghost_is[...] = 1.0 / scores
     ghost_it[...] = wide(inv_total)
-    message = scores * (LABELS * inv_total)
+    ghost_m[...] = scores * (LABELS * inv_total)
     for d in range(6):
-        face = message[d * 64 : d * 64 + 64]
+        face = ghost_m[pl.ds(d * 128, 64)]
         put(inc, (0, d), d // 2, d % 2 == 1, jnp.where(outside[d], 1.0, face))
 
+    def line_of(d, e):
+        return pl.ds(768 + edge_at(d, e) * 8, 8)
+
+    for d in range(6):
+        near = ghost_m[pl.ds(d * 128, 64)]
+        value = ghost_u[pl.ds(d * 128, 64)] * ghost_m[pl.ds(d * 128 + 64, 64)]
+        p, r = [axis for axis in range(3) if axis != d // 2]
+        for e in (2 * p, 2 * p + 1):
+            line = jnp.where(outside[e], 1.0, ghost_m[line_of(d, e)])
+            if e % 2 == 0:
+                value = value * jnp.concatenate([line, near[:56]], axis=0)
+            else:
+                value = value * jnp.concatenate([near[8:], line], axis=0)
+        for e in (2 * r, 2 * r + 1):
+            side[d, e % 2] = turn(near, 1 - 2 * (e % 2))
+            line = jnp.where(outside[e], 1.0, ghost_m[line_of(d, e)])
+            side[d, e % 2, pl.ds(0 if e % 2 == 0 else 7, 8, stride=8)] = line
+            value = value * side[d, e % 2]
+        ghost_c[pl.ds(d * 64, 64)] = value
+    scores = dot(ghost_c[...], table[...])
+    inv_total = 1.0 / lanes(scores)
+    ghost_is2[...] = 1.0 / scores
+    ghost_it2[...] = wide(inv_total)
+    ghost_m2 = scores * (LABELS * inv_total)
     for t in (1, 2):
-        faces = []
-        for d in range(6):
-            value = take(unary, (), d // 2, d % 2 == 0)
-            for e in range(6):
-                if e != d ^ 1:
-                    value = value * take(inc, (t - 1, e), d // 2, d % 2 == 0)
-            faces.append(value.astype(BF16))
-        scores = dot(jnp.concatenate(faces, axis=0), table[...])
-        message = scores * (LABELS / lanes(scores))
-        copies = [send(t, d, neighbour[d], message[d * 64 : d * 64 + 64]) for d in range(6)]
+        if t == 2:
+            faces = []
+            for d in range(6):
+                value = take(unary, (), d // 2, d % 2 == 0)
+                for e in range(6):
+                    if e != d ^ 1:
+                        value = value * take(inc, (t - 1, e), d // 2, d % 2 == 0)
+                faces.append(value.astype(BF16))
+            scores = dot(jnp.concatenate(faces, axis=0), table[...])
+            message = scores * (LABELS / lanes(scores))
+            copies = [send(0, d, neighbour[d], message[d * 64 : d * 64 + 64]) for d in range(6)]
 
         def messages(x, _, t=t):
             values, _ = cavities(unary[x + 1], [inc[t - 1, d, x + 1] for d in range(6)])
@@ -222,11 +297,15 @@
             return 0
 
         lax.fori_loop(0, 8, messages, 0, unroll=True)
-        for copy in copies:
-            copy.wait_recv()
-        for d in range(6):
-            face = in_face[t, d].astype(F32)
-            put(inc, (t, d), d // 2, d % 2 == 1, jnp.where(outside[d], 1.0, face))
+        if t == 1:
+            for d in range(6):
+                face = ghost_m2[d * 64 : d * 64 + 64]
+                put(inc, (1, d), d // 2, d % 2 == 1, jnp.where(outside[d], 1.0, face))
+    for copy in copies:
+        copy.wait_recv()
+    for d in range(6):
+        face = in_face[0, d].astype(F32)
+        put(inc, (2, d), d // 2, d % 2 == 1, jnp.where(outside[d], 1.0, face))
 
     loads[2].wait()
     empty = jnp.zeros((64, LABELS), F32)
@@ -246,7 +325,7 @@
         return 0
 
     lax.fori_loop(0, 8, beliefs, 0, unroll=True)
-    copies = [send(3, d, neighbour[d ^ 1], take(log_grad, (), d // 2, d % 2 == 1)) for d in range(6)]
+    copies = [send(1, d, neighbour[d ^ 1], take(log_grad, (), d // 2, d % 2 == 1)) for d in range(6)]
 
     place = lax.rem(lax.broadcasted_iota(jnp.int32, (64, LABELS), 0), 8)
     border = jnp.zeros((8, LABELS), F32)
@@ -272,10 +351,8 @@
 
     pair[...] = jnp.zeros_like(pair)
 
-    for t in (1, 0):
-        read = last_grads if t == 1 else grads_of(1)
-
-        def backward(x, _, t=t, read=read):
+    def backward(t, read):
+        for x in range(8):
             total = None
             for d in range(6):
                 grad = arrived(read, d, x)
@@ -286,71 +363,93 @@
                 parts[t, d, x + 1] = part
                 total = part if total is None else total + part
             whole[t, x + 1] = total
-            return 0
-
-        lax.fori_loop(0, 8, backward, 0, unroll=True)
-
-        def pair_terms(d, _, t=t):
+        for d in range(6):
             pair[...] += dot_rows(
                 cav16[t, d].reshape(512, LABELS), sgrad16[d].reshape(512, LABELS)
             )
-            return 0
-
-        lax.fori_loop(0, 6, pair_terms, 0, unroll=True)
-        for copy in copies:
-            copy.wait_recv()
-        rounded, factors_at = [], []
+
+    def backward_faces(t, stage):
+        rounded, at = [], []
         for d in range(6):
             upper = d % 2 == 0
-            grad = jnp.where(outside[d ^ 1], 0.0, in_face[4 - t, d].astype(F32))
+            grad = jnp.where(outside[d ^ 1], 0.0, in_face[stage, d].astype(F32))
             score_grad = grad * take(inv_s, (t, d), d // 2, upper)
             score_grad -= lanes(grad) * take(inv_t, (t, d), d // 2, upper)
             rounded.append(score_grad.astype(BF16))
-            factors_at.append(take(cav, (t, d), d // 2, upper))
+            at.append(take(cav, (t, d), d // 2, upper))
         rounded = jnp.concatenate(rounded, axis=0)
         back = dot(rounded, table_t[...])
         for d in range(6):
             upper = d % 2 == 0
-            part = back[d * 64 : d * 64 + 64] * factors_at[d]
+            part = back[d * 64 : d * 64 + 64] * at[d]
             put(parts, (t, d), d // 2, upper, part)
             put(whole, (t,), d // 2, upper, take(whole, (t,), d // 2, upper) + part)
-        copies = []
-        edge = []
-        for d in range(6):
-            upper = d % 2 == 1
-            grad = take(whole, (t,), d // 2, upper) - take(parts, (t, d ^ 1), d // 2, upper)
-            copies.append(send(5 - t, d, neighbour[d ^ 1], grad))
-            edge.append(grad)
-        at = jnp.concatenate(factors_at, axis=0).astype(BF16)
-        pair[...] += dot_rows(at, rounded)
+        return at, rounded
+
+    def leaving(t):
+        return [
+            take(whole, (t,), d // 2, d % 2 == 1) - take(parts, (t, d ^ 1), d // 2, d % 2 == 1)
+            for d in range(6)
+        ]
+
+    backward(1, last_grads)
+    for copy in copies:
+        copy.wait_recv()
+    at, rounded = backward_faces(1, 1)
+    edge = leaving(1)
+    copies = [send(2, d, neighbour[d ^ 1], edge[d]) for d in range(6)]
+    pair[...] += dot_rows(jnp.concatenate(at, axis=0).astype(BF16), rounded)
+
+    grad = jnp.concatenate([jnp.where(outside[d], 0.0, edge[d]) for d in range(6)], axis=0)
+    score_grad = grad * ghost_is2[...] - lanes(grad) * ghost_it2[...]
+    rounded = score_grad.astype(BF16)
+    pair[...] += dot_rows(ghost_c[...].astype(BF16), rounded)
+    beyond = dot(rounded, table_t[...]) * ghost_c[...]
+
+    backward(0, grads_of(1))
 
     read = grads_of(0)
 
-    def first_grads(x, _):
+    def first_grad(x):
         grad = arrived(read, 0, x)
         for d in range(1, 6):
             grad += arrived(read, d, x)
-        log_sum = grad * inv_s1[x + 1] - lanes(grad) * inv_t1[x + 1]
-        rounded = log_sum.astype(BF16)
-        sgrad16[0, x] = rounded
-        back = dot(rounded, table_t[...]) * unary[x + 1]
-        ug[x + 1] = log_grad[x + 1] + whole[1, x + 1] + whole[0, x + 1] + back
+        score_grad = grad * inv_s1[x + 1] - lanes(grad) * inv_t1[x + 1]
+        return score_grad.astype(BF16)
+
+    for x in range(8):
+        sgrad16[0, x] = first_grad(x)
         cav16[0, 0, x] = unary[x + 1].astype(BF16)
-        return 0
-
-    lax.fori_loop(0, 8, first_grads, 0, unroll=True)
     pair[...] += dot_rows(cav16[0, 0].reshape(512, LABELS), sgrad16[0].reshape(512, LABELS))
-    grad = jnp.concatenate([jnp.where(outside[d], 0.0, edge[d]) for d in range(6)], axis=0)
+
+    edge = leaving(0)
+    lines = [None] * len(EDGES)
+
+    def add_line(d, e, value):
+        k = edge_at(d, e)
+        value = jnp.where(outside[e], 0.0, value)
+        lines[k] = value if lines[k] is None else lines[k] + value
+
+    for d in range(6):
+        here = beyond[d * 64 : d * 64 + 64]
+        near = jnp.where(outside[d], 0.0, edge[d])
+        p, r = [axis for axis in range(3) if axis != d // 2]
+        near += jnp.concatenate([here[8:], border], axis=0)
+        add_line(d, 2 * p, here[:8])
+        near += jnp.concatenate([border, here[:56]], axis=0)
+        add_line(d, 2 * p + 1, here[56:])
+        near += jnp.where(place == 7, 0.0, turn(here, -1))
+        near += jnp.where(place == 0, 0.0, turn(here, 1))
+        side[d, 0] = here
+        add_line(d, 2 * r, side[d, 0, pl.ds(0, 8, stride=8)])
+        add_line(d, 2 * r + 1, side[d, 0, pl.ds(7, 8, stride=8)])
+        ghost_g[pl.ds(d * 128, 64)] = near
+        ghost_g[pl.ds(d * 128 + 64, 64)] = here
+    for k in range(len(EDGES)):
+        ghost_g[pl.ds(768 + k * 8, 8)] = lines[k]
+    grad = ghost_g[...]
     score_grad = grad * ghost_is[...] - lanes(grad) * ghost_it[...]
-    pair[...] += dot_rows(ghost_u[...], score_grad.astype(BF16))
-
-    def copy_to(src, dst, ss, rs, target):
-        copy = pltpu.make_async_remote_copy(
-            src_ref=src, dst_ref=dst, send_sem=ss, recv_sem=rs, device_id=target, device_id_type=MESH
-        )
-        copy.start()
-        started.append(copy)
-        return copy
+    pair[...] += dot_rows(ghost_u[...].astype(BF16), score_grad.astype(BF16))
 
     height = LABELS // firsts
 
@@ -358,7 +457,7 @@
         return pl.ds(pl.multiple_of(j * height, height), height)
 
     sends = [
-        copy_to(
+        send_from(
             pair.at[rows_of(lax.rem(first_id + k, firsts))], part1.at[k - 1],
             s1_ss.at[k - 1], s1_rs.at[k - 1], first_peer(k),
         )
@@ -367,10 +466,30 @@
 
     for copy in copies:
         copy.wait_recv()
+    backward_faces(0, 2)
+    edge = leaving(0)
+    copies = [send(3, d, neighbour[d ^ 1], edge[d]) for d in range(6)]
+
+    for copy in sends:
+        copy.wait_recv()
+    mine = pair[rows_of(first_id)]
+    for k in range(1, firsts):
+        mine += part1[k - 1]
+    part2[second_id] = mine.astype(BF16)
+    own = part2.at[second_id]
+    sends = [
+        send_from(own, own, s2_ss.at[k - 1], s2_rs.at[k - 1], second_peer(k))
+        for k in range(1, seconds)
+    ]
+    for x in range(8):
+        back = dot(first_grad(x), table_t[...]) * unary[x + 1]
+        ug[x + 1] = log_grad[x + 1] + whole[1, x + 1] + whole[0, x + 1] + back
+    for copy in copies:
+        copy.wait_recv()
     rounded = []
     for d in range(6):
         upper = d % 2 == 0
-        grad = jnp.where(outside[d ^ 1], 0.0, in_face[5, d].astype(F32))
+        grad = jnp.where(outside[d ^ 1], 0.0, in_face[3, d].astype(F32))
         score_grad = grad * take(inv_s1, (), d // 2, upper)
         score_grad -= lanes(grad) * take(inv_t1, (), d // 2, upper)
         rounded.append(score_grad.astype(BF16))
@@ -384,21 +503,10 @@
 
     for copy in sends:
         copy.wait_recv()
-    mine = pair[rows_of(first_id)]
-    for k in range(1, firsts):
-        mine += part1[k - 1]
-    part2[second_id] = mine.astype(BF16)
-    own = part2.at[second_id]
-    sends = [
-        copy_to(own, own, s2_ss.at[k - 1], s2_rs.at[k - 1], second_peer(k))
-        for k in range(1, seconds)
-    ]
-    for copy in sends:
-        copy.wait_recv()
     final[rows_of(first_id)] = jnp.sum(part2[...].astype(F32), axis=0)
     here = final.at[rows_of(first_id)]
     sends = [
-        copy_to(here, here, s3_ss.at[k - 1], s3_rs.at[k - 1], first_peer(k))
+        send_from(here, here, s3_ss.at[k - 1], s3_rs.at[k - 1], first_peer(k))
         for k in range(1, firsts)
     ]
     for copy in sends:
@@ -448,18 +556,26 @@
             vmem((6, *slabs), BF16),
             vmem((LABELS, LABELS), F32),
             vmem(padded, F32),
-            vmem((6, 6, 64, LABELS), BF16),
-            vmem((6, 6, 64, LABELS), BF16),
-            vmem((384, LABELS), BF16),
-            vmem((384, LABELS), F32),
-            vmem((384, LABELS), F32),
+            vmem((4, 6, 64, LABELS), BF16),
+            vmem((4, 6, 64, LABELS), BF16),
+            *[vmem((GHOSTS, LABELS), F32)] * 5,
+            *[vmem((384, LABELS), F32)] * 3,
+            vmem((6, 2, 64, LABELS), F32),
+            vmem((len(EDGES), 8, LABELS), F32),
+            vmem((len(EDGES), 8, LABELS), F32),
+            vmem((6, 128, LABELS), BF16),
+            vmem((6, 128, LABELS), BF16),
             vmem((firsts - 1, height, LABELS), F32),
             vmem((seconds, height, LABELS), BF16),
             vmem((LABELS, LABELS), F32),
             dma((3,)),
             dma((2,)),
-            dma((6, 6)),
-            dma((6, 6)),
+            dma((4, 6)),
+            dma((4, 6)),
+            dma((6,)),
+            dma((6,)),
+            dma((len(EDGES),)),
+            dma((len(EDGES),)),
             dma((firsts - 1,)),
             dma((firsts - 1,)),
             dma((seconds - 1,)),

time: 51.7 us -> 47.4 us (0.917)
  Pallas kernels: 48.6 us -> 44.3 us
    pallas_call x1, Pallas kernels: 48.6 us -> 44.3 us  [on_device(): pl.pallas_call(kernel, out_shape=(jax.ShapeDtypeStruct(slabs, F32), jax.S...]
where the time goes in v3:
time: 47.4 us; the launch traced here: 47.2 us
  Pallas kernels  44.3 us (93%)
  local copies, waits for them, and re-layouts  2.34 us (5%)
  between operations  0.65 us (1%)
    pallas_call x1, Pallas kernels, on_device(): pl.pallas_call(kernel, out_shape=(jax.ShapeDtypeStruct(slabs, F32), jax.S...  44.3 us
    unnamed x4, local copies, waits for them, and re-layouts  2.34 us

profile of v3, /device:TPU:1, one launch (start us, length us, event | category | flops | bytes accessed | tf_op | source)
XLA Modules:
  0.0 47.2 jit_solution(10094855803242050056)
XLA Ops:
  0.6 44.3 %shard_map.50 = (f32[8,64,128]{2,1,0:T(8,128)}, f32[128,128]{1,0:T(8,128)}) custom-call(s32[8,64,128]{2,1,0:T(8,128)} %bitcast.3, s32[128,128]{1,0:T(8,128)} %pot_hbm.1, bf16[8,64,128]{2,1,0:T(8,128)(2,1)} %bitcast.5), custom_call_target="tpu_custom_call" | custom-call | tf_op jit(solution)/shard_map/pallas_call | solution.py:531
  44.9 0.0 copy-start
  44.9 1.7 %copy.7 = f32[8,8,8,128]{3,2,1,0:T(8,128)} copy(f32[8,8,8,128]{3,2,1,0:T(8,128)} %bitcast.4) | data formatting | bytes 524288
  46.6 0.0 copy-done
  46.6 0.6 %copy.8 = f32[128,128]{1,0:T(8,128)} copy(f32[128,128]{1,0:T(8,128)S(1)} %copy-done) | data formatting | bytes 131072
Async XLA Ops:
  44.9 1.7 %copy-start = (f32[128,128]{1,0:T(8,128)S(1)}, f32[128,128]{1,0:T(8,128)}, u32[]{:S(2)}) copy-start(f32[128,128]{1,0:T(8,128)} %get-tuple-element.9) | copy-start | bytes 196612

commit v4 on v3

--- a/solution.py
+++ b/solution.py
@@ -139,12 +139,11 @@
     for place in neighbour + across:
         pl.semaphore_signal(barrier, inc=1, device_id=place, device_id_type=MESH)
         met += 1
-    for k in range(1, firsts):
-        pl.semaphore_signal(barrier, inc=1, device_id=first_peer(k), device_id_type=MESH)
-        met += 1
-    for k in range(1, seconds):
-        pl.semaphore_signal(barrier, inc=1, device_id=second_peer(k), device_id_type=MESH)
-        met += 1
+    for dy in (-1, 1):
+        for dz in (-2, 2):
+            place = (gx, lax.rem(gy + dy + ny, ny), lax.rem(gz + dz + nz, nz))
+            pl.semaphore_signal(barrier, inc=1, device_id=place, device_id_type=MESH)
+            met += 1
 
     started = []
 
@@ -519,6 +518,22 @@
     store2.start()
     store.wait()
     store2.wait()
+
+
+def finish(ug, pg, ug_out, pg_out, ug_held, pg_held, sem):
+    moves = [(pg, pg_held, pg_out)]
+    for x in range(0, 8, 4):
+        part = pl.ds(x, 4)
+        moves.append((ug.at[part], ug_held.at[part], ug_out.at[part]))
+    loads = [pltpu.make_async_copy(a, b, sem.at[0, k]) for k, (a, b, c) in enumerate(moves)]
+    stores = [pltpu.make_async_copy(b, c, sem.at[1, k]) for k, (a, b, c) in enumerate(moves)]
+    for load in loads:
+        load.start()
+    for load, store in zip(loads, stores):
+        load.wait()
+        store.start()
+    for store in stores:
+        store.wait()
 
 
 def on_device(unary_q, potential_q, belief_grad):
@@ -587,6 +602,16 @@
             collective_id=0, has_side_effects=True, vmem_limit_bytes=60 * 2**20
         ),
     )(unary_q.reshape(slabs), potential_q, belief_grad.reshape(slabs))
+    unary_grad, potential_grad = pl.pallas_call(
+        finish,
+        out_shape=(
+            jax.ShapeDtypeStruct(slabs, F32),
+            jax.ShapeDtypeStruct((LABELS, LABELS), F32),
+        ),
+        in_specs=[pl.BlockSpec(memory_space=pltpu.HBM)] * 2,
+        out_specs=(pl.BlockSpec(memory_space=pltpu.HBM),) * 2,
+        scratch_shapes=[vmem(slabs, F32), vmem((LABELS, LABELS), F32), dma((2, 3))],
+    )(unary_grad, potential_grad)
     return unary_grad.reshape(unary_q.shape), potential_grad
 
 

time: 47.4 us -> 46.2 us (0.975)
  local copies, waits for them, and re-layouts: 2.34 us -> 0 us
  Pallas kernels: 44.3 us -> 45.4 us
    unnamed x4 -> x0, local copies, waits for them, and re-layouts: 2.34 us -> none
    pallas_call x0 -> x1, Pallas kernels: none -> 1.71 us  [on_device(): pl.pallas_call(finish, out_shape=(jax.ShapeDtypeStruct(slabs, F32), jax.S...]
    pallas_call x1, Pallas kernels: 44.3 us -> 43.7 us  [on_device(): pl.pallas_call(kernel, out_shape=(jax.ShapeDtypeStruct(slabs, F32), jax.S...]
where the time goes in v4:
time: 46.2 us; the launch traced here: 46.1 us
  Pallas kernels  45.4 us (98%)
  between operations  0.64 us (1%)
    pallas_call x1, Pallas kernels, on_device(): pl.pallas_call(kernel, out_shape=(jax.ShapeDtypeStruct(slabs, F32), jax.S...  43.7 us
    pallas_call x1, Pallas kernels, on_device(): pl.pallas_call(finish, out_shape=(jax.ShapeDtypeStruct(slabs, F32), jax.S...  1.71 us

profile of v4, /device:TPU:1, one launch (start us, length us, event | category | flops | bytes accessed | tf_op | source)
XLA Modules:
  0.0 46.1 jit_solution(17153959341019544673)
XLA Ops:
  0.6 43.7 %shard_map.50 = (f32[8,64,128]{2,1,0:T(8,128)}, f32[128,128]{1,0:T(8,128)}) custom-call(s32[8,64,128]{2,1,0:T(8,128)} %bitcast.3, s32[128,128]{1,0:T(8,128)} %pot_hbm.1, bf16[8,64,128]{2,1,0:T(8,128)(2,1)} %bitcast.4), custom_call_target="tpu_custom_call" | custom-call | tf_op jit(solution)/shard_map/pallas_call | solution.py:546
  44.4 1.7 %shard_map.51 = (f32[8,64,128]{2,1,0:T(8,128)}, f32[128,128]{1,0:T(8,128)}) custom-call(f32[8,64,128]{2,1,0:T(8,128)} %get-tuple-element.6.ug, f32[128,128]{1,0:T(8,128)} %get-tuple-element.7.pg), custom_call_target="tpu_custom_call" | custom-call | tf_op jit(solution)/shard_map/pallas_call | solution.py:605

commit v5 on v4

--- a/solution.py
+++ b/solution.py
@@ -119,13 +119,17 @@
     second_id = gy * (nz // 2) + gz // 2
     seconds = ny * (nz // 2)
 
-    def first_peer(k):
-        j = lax.rem(first_id + k, firsts)
-        return (j // 2, gy, gz - core + lax.rem(j, 2))
-
-    def second_peer(k):
-        j = lax.rem(second_id + k, seconds)
-        return (gx, j // (nz // 2), lax.rem(j, nz // 2) * 2 + core)
+    xs = [lax.rem(gx + step, nx) for step in range(nx)]
+    ys = [lax.rem(gy + step, ny) for step in range(ny)]
+    zs = [lax.rem(gz + step, nz) for step in range(0, nz, 2)]
+    other = 1 - core
+    first_peers = [
+        ((x, gy, gz + flip * (other - core)), x * 2 + (other if flip else core))
+        for x in xs for flip in range(2)
+    ][1:]
+    steps = [(j, k) for j in range(ny) for k in range(nz // 2)][1:]
+    steps.sort(key=lambda at: -2 * min(at[1], nz // 2 - at[1]) - min(at[0] % 4, 4 - at[0] % 4))
+    second_peers = [(gx, ys[j], zs[k]) for j, k in steps]
 
     loads = [
         pltpu.make_async_copy(q_hbm, q, in_sem.at[0]),
@@ -168,7 +172,6 @@
         return 0
 
     lax.fori_loop(0, 8, factors, 0, unroll=True)
-    pl.semaphore_wait(barrier, met)
     copies = []
 
     def send_from(src, dst, ss, rs, target):
@@ -189,11 +192,14 @@
             for x in range(8):
                 row = pl.ds(near[0] * 8 + near[1], 1)
                 line_out[k, pl.ds(x, 1)] = unary[x + 1, row]
-        copies.append(send_from(line_out.at[k], line_in.at[k], line_ss.at[k], line_rs.at[k], across[k]))
     for d in range(6):
         near, behind = (7, 6) if d % 2 == 0 else (0, 1)
         halo_out[d, pl.ds(0, 64)] = layer(unary, d // 2, near).astype(BF16)
         halo_out[d, pl.ds(64, 64)] = layer(unary, d // 2, behind).astype(BF16)
+    pl.semaphore_wait(barrier, met)
+    for k in reversed(range(len(EDGES))):
+        copies.append(send_from(line_out.at[k], line_in.at[k], line_ss.at[k], line_rs.at[k], across[k]))
+    for d in reversed(range(6)):
         copies.append(send_from(halo_out.at[d], halo_in.at[d], halo_ss.at[d], halo_rs.at[d], neighbour[d]))
 
     loads[1].wait()
@@ -280,7 +286,7 @@
                 faces.append(value.astype(BF16))
             scores = dot(jnp.concatenate(faces, axis=0), table[...])
             message = scores * (LABELS / lanes(scores))
-            copies = [send(0, d, neighbour[d], message[d * 64 : d * 64 + 64]) for d in range(6)]
+            copies = [send(0, d, neighbour[d], message[d * 64 : d * 64 + 64]) for d in reversed(range(6))]
 
         def messages(x, _, t=t):
             values, _ = cavities(unary[x + 1], [inc[t - 1, d, x + 1] for d in range(6)])
@@ -324,7 +330,7 @@
         return 0
 
     lax.fori_loop(0, 8, beliefs, 0, unroll=True)
-    copies = [send(1, d, neighbour[d ^ 1], take(log_grad, (), d // 2, d % 2 == 1)) for d in range(6)]
+    copies = [send(1, d, neighbour[d ^ 1], take(log_grad, (), d // 2, d % 2 == 1)) for d in reversed(range(6))]
 
     place = lax.rem(lax.broadcasted_iota(jnp.int32, (64, LABELS), 0), 8)
     border = jnp.zeros((8, LABELS), F32)
@@ -456,11 +462,8 @@
         return pl.ds(pl.multiple_of(j * height, height), height)
 
     sends = [
-        send_from(
-            pair.at[rows_of(lax.rem(first_id + k, firsts))], part1.at[k - 1],
-            s1_ss.at[k - 1], s1_rs.at[k - 1], first_peer(k),
-        )
-        for k in range(1, firsts)
+        send_from(pair.at[rows_of(j)], part1.at[k], s1_ss.at[k], s1_rs.at[k], target)
+        for k, (target, j) in enumerate(first_peers)
     ]
 
     for copy in copies:
@@ -476,9 +479,10 @@
         mine += part1[k - 1]
     part2[second_id] = mine.astype(BF16)
     own = part2.at[second_id]
+    early = list(started)
     sends = [
-        send_from(own, own, s2_ss.at[k - 1], s2_rs.at[k - 1], second_peer(k))
-        for k in range(1, seconds)
+        send_from(own, own, s2_ss.at[k], s2_rs.at[k], target)
+        for k, target in enumerate(second_peers)
     ]
     for x in range(8):
         back = dot(first_grad(x), table_t[...]) * unary[x + 1]
@@ -499,23 +503,27 @@
         put(ug, (), d // 2, upper, take(ug, (), d // 2, upper) + part)
     store = pltpu.make_async_copy(ug.at[pl.ds(1, 8)], ug_out, out_sem.at[0])
     store.start()
+    for copy in early:
+        copy.wait_send()
+    factor = jnp.exp(pot[...].astype(F32) / 64.0) * (LABELS / math.sqrt(CELLS))
 
     for copy in sends:
         copy.wait_recv()
     final[rows_of(first_id)] = jnp.sum(part2[...].astype(F32), axis=0)
     here = final.at[rows_of(first_id)]
-    sends = [
-        send_from(here, here, s3_ss.at[k - 1], s3_rs.at[k - 1], first_peer(k))
-        for k in range(1, firsts)
+    gathers = [
+        send_from(here, here, s3_ss.at[k], s3_rs.at[k], target)
+        for k, (target, _) in enumerate(first_peers)
     ]
     for copy in sends:
-        copy.wait_recv()
-    factor = jnp.exp(pot[...].astype(F32) / 64.0)
-    for copy in started:
         copy.wait_send()
-    pair[...] = factor * final[...] * (LABELS / math.sqrt(CELLS))
+    for copy in gathers:
+        copy.wait_recv()
+    pair[...] = factor * final[...]
     store2 = pltpu.make_async_copy(pair, pg_out, out_sem.at[1])
     store2.start()
+    for copy in gathers:
+        copy.wait_send()
     store.wait()
     store2.wait()
 

time: 46.2 us -> 46.1 us (level)
  no operation moved by 1% of the time
where the time goes in v5:
time: 46.1 us; the launch traced here: 45.9 us
  Pallas kernels  45.3 us (98%)
  between operations  0.64 us (1%)
    pallas_call x1, Pallas kernels, on_device(): pl.pallas_call(kernel, out_shape=(jax.ShapeDtypeStruct(slabs, F32), jax.S...  43.6 us
    pallas_call x1, Pallas kernels, on_device(): pl.pallas_call(finish, out_shape=(jax.ShapeDtypeStruct(slabs, F32), jax.S...  1.71 us

profile of v5, /device:TPU:1, one launch (start us, length us, event | category | flops | bytes accessed | tf_op | source)
XLA Modules:
  0.0 45.9 jit_solution(15127263352440458870)
XLA Ops:
  0.6 43.6 %shard_map.50 = (f32[8,64,128]{2,1,0:T(8,128)}, f32[128,128]{1,0:T(8,128)}) custom-call(s32[8,64,128]{2,1,0:T(8,128)} %bitcast.3, s32[128,128]{1,0:T(8,128)} %pot_hbm.1, bf16[8,64,128]{2,1,0:T(8,128)(2,1)} %bitcast.4), custom_call_target="tpu_custom_call" | custom-call | tf_op jit(solution)/shard_map/pallas_call | solution.py:554
  44.2 1.7 %shard_map.51 = (f32[8,64,128]{2,1,0:T(8,128)}, f32[128,128]{1,0:T(8,128)}) custom-call(f32[8,64,128]{2,1,0:T(8,128)} %get-tuple-element.6.ug, f32[128,128]{1,0:T(8,128)} %get-tuple-element.7.pg), custom_call_target="tpu_custom_call" | custom-call | tf_op jit(solution)/shard_map/pallas_call | solution.py:613
